TPU v7x, 32 devices: a whole 2x2x4 slice. The times are simulated.
32 devices in a mesh: seq: 8 (over z, y), frame: 4 (over x, core).
Axes of the slice: x: 2, y: 2, z: 4, core: 2. Of those that a mesh axis runs over, the one named last changes fastest.
Arguments:
- latents: float32 [24, 64, 1536], P('seq', 'frame'), may hold values from -6 to 6
- patch_feats: float32 [24, 2, 4, 256, 1536], P('seq', None, 'frame'), may hold values from -6 to 6
- image_counts: int32 [24], P('seq'), may hold values from 0 to 8, as said below
- time_index: int32 [24, 8], P('seq'), may hold values from 0 to 7
- query_proj: float32 [1536, 1536], P(('seq', 'frame')), may hold values from -0.15625 to 0.15625
- key_proj: float32 [1536, 1536], P(('seq', 'frame')), may hold values from -0.15625 to 0.15625
- value_proj: float32 [1536, 1536], P(('seq', 'frame')), may hold values from -0.15625 to 0.15625
- out_proj: float32 [1536, 1536], P(('seq', 'frame')), may hold values from -0.625 to 0.625
- up_proj: float32 [1536, 6144], P(('seq', 'frame')), may hold values from -0.15625 to 0.15625
- down_proj: float32 [6144, 1536], P(('seq', 'frame')), may hold values from -0.078125 to 0.078125
- media_gain: float32 [1536], P(('seq', 'frame')), may hold values from 0.1 to 1.9
- media_bias: float32 [1536], P(('seq', 'frame')), may hold values from -4 to 4
- latent_gain: float32 [1536], P(('seq', 'frame')), may hold values from 0.1 to 1.9
- latent_bias: float32 [1536], P(('seq', 'frame')), may hold values from -4 to 4
- feed_gain: float32 [1536], P(('seq', 'frame')), may hold values from 0.1 to 1.9
- feed_bias: float32 [1536], P(('seq', 'frame')), may hold values from -4 to 4
- time_table: float32 [8, 1536], P(None, ('seq', 'frame')), may hold values from -6 to 6
- out_cotangent: float32 [24, 64, 1536], P('seq', 'frame'), may hold values from -6 to 6
Outputs:
- new_latents: float32 [24, 64, 1536], P('seq', 'frame')
- latent_grads: float32 [24, 64, 1536], P('seq', 'frame')
- patch_grads: float32 [24, 2, 4, 256, 1536], P('seq', None, 'frame')
- grad_query: float32 [1536, 1536], P(('seq', 'frame'))
- grad_key: float32 [1536, 1536], P(('seq', 'frame'))
- grad_value: float32 [1536, 1536], P(('seq', 'frame'))
- grad_out: float32 [1536, 1536], P(('seq', 'frame'))
- grad_up: float32 [1536, 6144], P(('seq', 'frame'))
- grad_down: float32 [6144, 1536], P(('seq', 'frame'))
- grad_media_gain: float32 [1536], P(('seq', 'frame'))
- grad_media_bias: float32 [1536], P(('seq', 'frame'))
- grad_latent_gain: float32 [1536], P(('seq', 'frame'))
- grad_latent_bias: float32 [1536], P(('seq', 'frame'))
- grad_feed_gain: float32 [1536], P(('seq', 'frame'))
- grad_feed_bias: float32 [1536], P(('seq', 'frame'))
- grad_time_table: float32 [8, 1536], P(None, ('seq', 'frame'))
Inputs may be any that keep to these rules, and one draw needn't show every extreme that they name: `image_counts`: each aligned block of 3 sequences holds one with 4 images or more, and some sequence has 8.
All inputs are finite; a program needn't handle non-finite values.
Results may differ from a plain program's by a relative error of at most 0.0003.
Values sent between devices are 32-bit elements; how exact they have to be, the bound alone decides.
A program may use at most 512 MiB of HBM per device.

v0:
```python
import math

import jax
import jax.numpy as jnp
from jax import lax
from jax.sharding import PartitionSpec as P

HEADS = 16


HIGHEST = lax.Precision.HIGHEST
EPSILON = 1e-05
MASKED = -1e30


def product(left, right):
    return jnp.dot(left, right, precision=HIGHEST, preferred_element_type=jnp.float32)


def product_tn(left, right):
    return lax.dot_general(
        left, right, (((0,), (0,)), ((), ())), precision=HIGHEST, preferred_element_type=jnp.float32
    )


def product_nt(left, right):
    return lax.dot_general(
        left, right, (((1,), (1,)), ((), ())), precision=HIGHEST, preferred_element_type=jnp.float32
    )


def flatten(values):
    return values.reshape(-1, values.shape[-1])


def norm_forward(values, gain_vec, bias_vec):
    centred = values - jnp.mean(values, axis=-1, keepdims=True)
    inv_std = lax.rsqrt(jnp.mean(centred * centred, axis=-1, keepdims=True) + EPSILON)
    unit_vals = centred * inv_std
    return (unit_vals * gain_vec + bias_vec, unit_vals, inv_std)


def norm_backward(incoming, unit_vals, inv_std, gain_vec):
    scaled = incoming * gain_vec
    result = inv_std * (
        scaled
        - jnp.mean(scaled, axis=-1, keepdims=True)
        - unit_vals * jnp.mean(scaled * unit_vals, axis=-1, keepdims=True)
    )
    flat_in = flatten(incoming)
    return (result, jnp.sum(flat_in * flatten(unit_vals), axis=0), jnp.sum(flat_in, axis=0))


def heads_last(stats):
    return jnp.transpose(stats, (0, 2, 1))[..., None]


def per_slot(action, operands):
    return lax.map(action, operands)


def body(
    latents,
    patch_feats,
    image_counts,
    time_index,
    query_proj,
    key_proj,
    value_proj,
    out_proj,
    up_proj,
    down_proj,
    media_gain,
    media_bias,
    latent_gain,
    latent_bias,
    feed_gain,
    feed_bias,
    time_table,
    out_cotangent,
):
    gathered = (
        lax.all_gather(query_proj, ("seq", "frame"), axis=0, tiled=True),
        lax.all_gather(key_proj, ("seq", "frame"), axis=0, tiled=True),
        lax.all_gather(value_proj, ("seq", "frame"), axis=0, tiled=True),
        lax.all_gather(out_proj, ("seq", "frame"), axis=0, tiled=True),
        lax.all_gather(up_proj, ("seq", "frame"), axis=0, tiled=True),
        lax.all_gather(down_proj, ("seq", "frame"), axis=0, tiled=True),
        lax.all_gather(media_gain, ("seq", "frame"), axis=0, tiled=True),
        lax.all_gather(media_bias, ("seq", "frame"), axis=0, tiled=True),
        lax.all_gather(latent_gain, ("seq", "frame"), axis=0, tiled=True),
        lax.all_gather(latent_bias, ("seq", "frame"), axis=0, tiled=True),
        lax.all_gather(feed_gain, ("seq", "frame"), axis=0, tiled=True),
        lax.all_gather(feed_bias, ("seq", "frame"), axis=0, tiled=True),
        lax.all_gather(time_table, ("seq", "frame"), axis=1, tiled=True),
    )
    (
        query_full,
        key_full,
        value_full,
        out_full,
        up_full,
        down_full,
        mgain_full,
        mbias_full,
        lgain_full,
        lbias_full,
        fgain_full,
        fbias_full,
        table_full,
    ) = gathered
    frame_index = lax.axis_index("frame")
    frame_count = lax.axis_size("frame")
    seq_local, lat_rows, model_width = latents.shape
    round_count = patch_feats.shape[1]
    patch_count = patch_feats.shape[3]
    slot_total = time_index.shape[1]
    table_rows = time_table.shape[0]
    latent_total = lat_rows * frame_count
    head_size = model_width // HEADS
    inv_root = 1.0 / math.sqrt(head_size)
    latent_all = lax.all_gather(latents, "frame", axis=1, tiled=True)
    latent_norm, latent_unit, latent_std = norm_forward(latent_all, lgain_full, lbias_full)
    row_start = frame_index * lat_rows
    own_norm = lax.dynamic_slice_in_dim(latent_norm, row_start, lat_rows, 1)
    own_unit = lax.dynamic_slice_in_dim(latent_unit, row_start, lat_rows, 1)
    own_std = lax.dynamic_slice_in_dim(latent_std, row_start, lat_rows, 1)
    queries = product(flatten(latent_norm), query_full).reshape(
        seq_local, latent_total, model_width
    )
    own_keys = product(flatten(own_norm), key_full).reshape(seq_local, lat_rows, model_width)
    own_values = product(flatten(own_norm), value_full).reshape(seq_local, lat_rows, model_width)
    slot_ids = jnp.arange(round_count, dtype=jnp.int32) * frame_count + frame_index
    present = slot_ids[None, :] < image_counts[:, None]
    picks = jnp.arange(slot_total, dtype=jnp.int32)[None, :] == slot_ids[:, None]
    slot_times = jnp.sum(jnp.where(picks[None, :, :], time_index[:, None, :], 0), axis=-1)
    one_hot = (
        slot_times.reshape(-1)[:, None] == jnp.arange(table_rows, dtype=jnp.int32)[None, :]
    ).astype(jnp.float32)
    slot_embed = product(one_hot, table_full)
    slot_feats = patch_feats.reshape(seq_local * round_count, patch_count, model_width)

    def media_forward(element):
        normed, unit_part, std_part = norm_forward(
            element[0] + element[1][None, :], mgain_full, mbias_full
        )
        return (normed, unit_part, std_part, product(normed, key_full), product(normed, value_full))

    media_norm, media_unit, media_std, media_keys, media_values = per_slot(
        media_forward, (slot_feats, slot_embed)
    )
    key_total = lat_rows + round_count * patch_count
    all_keys = jnp.concatenate(
        [own_keys, media_keys.reshape(seq_local, round_count * patch_count, model_width)], axis=1
    )
    all_values = jnp.concatenate(
        [own_values, media_values.reshape(seq_local, round_count * patch_count, model_width)],
        axis=1,
    )
    keep = jnp.concatenate(
        [jnp.ones((seq_local, lat_rows), dtype=bool), jnp.repeat(present, patch_count, axis=1)],
        axis=1,
    )
    query_four = queries.reshape(seq_local, latent_total, HEADS, head_size)
    key_four = all_keys.reshape(seq_local, key_total, HEADS, head_size)
    value_four = all_values.reshape(seq_local, key_total, HEADS, head_size)

    def masked_scores():
        raw_scores = (
            jnp.einsum(
                "bqhe,bkhe->bhqk",
                query_four,
                key_four,
                precision=HIGHEST,
                preferred_element_type=jnp.float32,
            )
            * inv_root
        )
        return jnp.where(keep[:, None, None, :], raw_scores, MASKED)

    scores = masked_scores()
    row_top = jnp.max(scores, axis=-1)
    expo = jnp.exp(scores - row_top[..., None])
    row_total = jnp.sum(expo, axis=-1)
    partial_out = jnp.einsum(
        "bhqk,bkhe->bqhe", expo, value_four, precision=HIGHEST, preferred_element_type=jnp.float32
    )
    glob_top = lax.pmax(row_top, "frame")
    ratio = jnp.exp(row_top - glob_top)
    glob_total, glob_out = lax.psum((row_total * ratio, partial_out * heads_last(ratio)), "frame")
    attended = glob_out / heads_last(glob_total)
    log_total = glob_top + jnp.log(glob_total)
    attended_flat = attended.reshape(seq_local, latent_total, model_width)
    own_attended = lax.dynamic_slice_in_dim(attended_flat, row_start, lat_rows, 1)
    middle = latents + product(flatten(own_attended), out_full).reshape(
        seq_local, lat_rows, model_width
    )
    feed_norm, feed_unit, feed_std = norm_forward(middle, fgain_full, fbias_full)
    hidden_pre = product(flatten(feed_norm), up_full)
    activated, gelu_pull = jax.vjp(jax.nn.gelu, hidden_pre)
    new_latents = middle + product(activated, down_full).reshape(seq_local, lat_rows, model_width)
    regathered = (
        lax.all_gather(query_proj, ("seq", "frame"), axis=0, tiled=True),
        lax.all_gather(key_proj, ("seq", "frame"), axis=0, tiled=True),
        lax.all_gather(value_proj, ("seq", "frame"), axis=0, tiled=True),
        lax.all_gather(out_proj, ("seq", "frame"), axis=0, tiled=True),
        lax.all_gather(up_proj, ("seq", "frame"), axis=0, tiled=True),
        lax.all_gather(down_proj, ("seq", "frame"), axis=0, tiled=True),
        lax.all_gather(media_gain, ("seq", "frame"), axis=0, tiled=True),
        lax.all_gather(media_bias, ("seq", "frame"), axis=0, tiled=True),
        lax.all_gather(latent_gain, ("seq", "frame"), axis=0, tiled=True),
        lax.all_gather(latent_bias, ("seq", "frame"), axis=0, tiled=True),
        lax.all_gather(feed_gain, ("seq", "frame"), axis=0, tiled=True),
        lax.all_gather(feed_bias, ("seq", "frame"), axis=0, tiled=True),
        lax.all_gather(time_table, ("seq", "frame"), axis=1, tiled=True),
    )
    query_back = regathered[0]
    key_back = regathered[1]
    value_back = regathered[2]
    out_back = regathered[3]
    up_back = regathered[4]
    down_back = regathered[5]
    mgain_back = regathered[6]
    lgain_back = regathered[8]
    fgain_back = regathered[10]
    cotangent = flatten(out_cotangent)
    grad_down = product_tn(activated, cotangent)
    grad_hidden = gelu_pull(product_nt(cotangent, down_back))[0]
    grad_up = product_tn(flatten(feed_norm), grad_hidden)
    grad_feed_norm = product_nt(grad_hidden, up_back).reshape(seq_local, lat_rows, model_width)
    grad_mid_norm, grad_fgain, grad_fbias = norm_backward(
        grad_feed_norm, feed_unit, feed_std, fgain_back
    )
    grad_middle = out_cotangent + grad_mid_norm
    grad_out_w = product_tn(flatten(own_attended), flatten(grad_middle))
    grad_own_att = product_nt(flatten(grad_middle), out_back).reshape(
        seq_local, lat_rows, model_width
    )
    grad_attended = lax.all_gather(grad_own_att, "frame", axis=1, tiled=True)
    grad_four = grad_attended.reshape(seq_local, latent_total, HEADS, head_size)
    delta_rows = jnp.einsum(
        "bqhe,bqhe->bhq", grad_four, attended, precision=HIGHEST, preferred_element_type=jnp.float32
    )
    probs = jnp.exp(masked_scores() - log_total[..., None])
    grad_probs = jnp.einsum(
        "bqhe,bkhe->bhqk",
        grad_four,
        value_four,
        precision=HIGHEST,
        preferred_element_type=jnp.float32,
    )
    grad_scores = probs * (grad_probs - delta_rows[..., None]) * inv_root
    grad_query_part = jnp.einsum(
        "bhqk,bkhe->bqhe",
        grad_scores,
        key_four,
        precision=HIGHEST,
        preferred_element_type=jnp.float32,
    ).reshape(seq_local, latent_total, model_width)
    grad_keys = jnp.einsum(
        "bhqk,bqhe->bkhe",
        grad_scores,
        query_four,
        precision=HIGHEST,
        preferred_element_type=jnp.float32,
    ).reshape(seq_local, key_total, model_width)
    grad_values = jnp.einsum(
        "bhqk,bqhe->bkhe", probs, grad_four, precision=HIGHEST, preferred_element_type=jnp.float32
    ).reshape(seq_local, key_total, model_width)
    grad_query_own = lax.psum_scatter(grad_query_part, "frame", scatter_dimension=1, tiled=True)
    grad_key_lat = flatten(grad_keys[:, :lat_rows])
    grad_value_lat = flatten(grad_values[:, :lat_rows])
    grad_key_media = grad_keys[:, lat_rows:].reshape(
        seq_local * round_count, patch_count, model_width
    )
    grad_value_media = grad_values[:, lat_rows:].reshape(
        seq_local * round_count, patch_count, model_width
    )
    grad_query_w = product_tn(flatten(own_norm), flatten(grad_query_own))
    grad_key_w = product_tn(flatten(own_norm), grad_key_lat) + product_tn(
        flatten(media_norm), flatten(grad_key_media)
    )
    grad_value_w = product_tn(flatten(own_norm), grad_value_lat) + product_tn(
        flatten(media_norm), flatten(grad_value_media)
    )
    grad_own_norm = (
        product_nt(flatten(grad_query_own), query_back)
        + product_nt(grad_key_lat, key_back)
        + product_nt(grad_value_lat, value_back)
    ).reshape(seq_local, lat_rows, model_width)
    grad_lat_in, grad_lgain, grad_lbias = norm_backward(
        grad_own_norm, own_unit, own_std, lgain_back
    )
    latent_grads = grad_middle + grad_lat_in

    def media_backward(element):
        normed_grad = product_nt(element[0], key_back) + product_nt(element[1], value_back)
        feats_grad, gain_part, bias_part = norm_backward(
            normed_grad, element[2], element[3], mgain_back
        )
        return (feats_grad, gain_part, bias_part, jnp.sum(feats_grad, axis=0))

    feats_grads, gain_parts, bias_parts, slot_sums = per_slot(
        media_backward, (grad_key_media, grad_value_media, media_unit, media_std)
    )
    grad_mgain = jnp.sum(gain_parts, axis=0)
    grad_mbias = jnp.sum(bias_parts, axis=0)
    grad_table = product_tn(one_hot, slot_sums)
    patch_grads = feats_grads.reshape(patch_feats.shape)
    summed = (
        lax.psum_scatter(grad_query_w, ("seq", "frame"), scatter_dimension=0, tiled=True),
        lax.psum_scatter(grad_key_w, ("seq", "frame"), scatter_dimension=0, tiled=True),
        lax.psum_scatter(grad_value_w, ("seq", "frame"), scatter_dimension=0, tiled=True),
        lax.psum_scatter(grad_out_w, ("seq", "frame"), scatter_dimension=0, tiled=True),
        lax.psum_scatter(grad_up, ("seq", "frame"), scatter_dimension=0, tiled=True),
        lax.psum_scatter(grad_down, ("seq", "frame"), scatter_dimension=0, tiled=True),
        lax.psum_scatter(grad_mgain, ("seq", "frame"), scatter_dimension=0, tiled=True),
        lax.psum_scatter(grad_mbias, ("seq", "frame"), scatter_dimension=0, tiled=True),
        lax.psum_scatter(grad_lgain, ("seq", "frame"), scatter_dimension=0, tiled=True),
        lax.psum_scatter(grad_lbias, ("seq", "frame"), scatter_dimension=0, tiled=True),
        lax.psum_scatter(grad_fgain, ("seq", "frame"), scatter_dimension=0, tiled=True),
        lax.psum_scatter(grad_fbias, ("seq", "frame"), scatter_dimension=0, tiled=True),
        lax.psum_scatter(grad_table, ("seq", "frame"), scatter_dimension=1, tiled=True),
    )
    return (
        new_latents,
        latent_grads,
        patch_grads,
        summed[0],
        summed[1],
        summed[2],
        summed[3],
        summed[4],
        summed[5],
        summed[6],
        summed[7],
        summed[8],
        summed[9],
        summed[10],
        summed[11],
        summed[12],
    )


def solution(mesh):
    return jax.shard_map(
        body,
        mesh=mesh,
        in_specs=(
            P("seq", "frame", None),
            P("seq", None, "frame", None, None),
            P("seq"),
            P("seq", None),
            P(("seq", "frame"), None),
            P(("seq", "frame"), None),
            P(("seq", "frame"), None),
            P(("seq", "frame"), None),
            P(("seq", "frame"), None),
            P(("seq", "frame"), None),
            P(("seq", "frame")),
            P(("seq", "frame")),
            P(("seq", "frame")),
            P(("seq", "frame")),
            P(("seq", "frame")),
            P(("seq", "frame")),
            P(None, ("seq", "frame")),
            P("seq", "frame", None),
        ),
        out_specs=(
            P("seq", "frame", None),
            P("seq", "frame", None),
            P("seq", None, "frame", None, None),
            P(("seq", "frame"), None),
            P(("seq", "frame"), None),
            P(("seq", "frame"), None),
            P(("seq", "frame"), None),
            P(("seq", "frame"), None),
            P(("seq", "frame"), None),
            P(("seq", "frame")),
            P(("seq", "frame")),
            P(("seq", "frame")),
            P(("seq", "frame")),
            P(("seq", "frame")),
            P(("seq", "frame")),
            P(None, ("seq", "frame")),
        ),
        check_vma=False,
    )
```

profile of v0, /device:TPU:0, one launch (start us, length us, event | category | flops | bytes accessed | tf_op | source)
XLA Modules:
  0.0 2957.2 jit_solution(3635141556530000793)
XLA Ops:
  10.0 43.9 %all-gather = f32[32,48,8]{1,2,0:T(8,128)S(1)} all-gather(f32[1,48,8]{1,2,0:T(8,128)} %bitcast.248), channel_id=1, replica_groups=mesh['seq'=8,'frame'=4] {'seq','frame'}, dimensions={0}, use_global_device_ids=true | all-gather | bytes 50688 | tf_op jit(solution)/shard_map/all_gather | solution.py:95
  61.1 38.6 %all-reduce.14 = (f32[1536]{0:T(1024)S(1)}, f32[1536]{0:T(1024)S(1)}, f32[1536]{0:T(1024)S(1)}, f32[1536]{0:T(1024)S(1)}, f32[1536]{0:T(1024)S(1)}, /*index=5*/f32[1536]{0:T(1024)S(1)}) all-reduce(f32[1536]{0:T(1024)S(1)} %dynamic-update-slice.1, f32[1536]{0:T(1024)S(1)} %dynamic-update-slice, ...), channel_id=1, replica_groups=mesh['seq'=8,'frame'=4] {'seq','frame'}, use_global_device_ids=true, to_apply=%add.2 | all-reduce | flops 9216 | bytes 73728
  126.1 74.0 %all-gather.14.cloned.1.call-done = f32[1536,1536]{1,0:T(8,128)} async-done(((f32[48,1536]{1,0:T(8,128)}), f32[1536,1536]{1,0:T(8,128)}) %all-gather.14.cloned.1.call-update) | async-done | bytes 9437200 | tf_op jit(solution)/shard_map/all_gather | solution.py:84
  200.1 83.4 %all-gather.12.cloned.1.call-done = f32[1536,1536]{1,0:T(8,128)} async-done(((f32[48,1536]{1,0:T(8,128)}), f32[1536,1536]{1,0:T(8,128)}) %all-gather.12.cloned.1.call-update) | async-done | bytes 9437200 | tf_op jit(solution)/shard_map/all_gather | solution.py:85
  302.6 187.9 %while.34 = (s32[]{:T(128)}, f32[6,256,1536]{2,1,0:T(8,128)}, f32[6,256,1536]{2,1,0:T(8,128)}, f32[6,256,1]{1,2,0:T(1,128)}, f32[6,256,1536]{2,1,0:T(8,128)}, /*...) while((s32[]{:T(128)}, f32[6,256,1536]{2,1,0:T(8,128)}, ...), condition=%wide.region_6.7_spmd, body=%wide.region_3.6_spmd.sunk | while | flops 14503772160 | bytes 61439200 | solution.py:59
  651.4 28.0 all-reduce.17.cloned.1.call-done
  683.0 81.3 %all-gather.18.cloned.1.call-done = f32[1536,1536]{1,0:T(8,128)} async-done(((f32[48,1536]{1,0:T(8,128)}), f32[1536,1536]{1,0:T(8,128)}) %all-gather.18.cloned.1.call-update) | async-done | bytes 9437200 | tf_op jit(solution)/shard_map/all_gather | solution.py:86
  773.4 207.4 %all-gather.20.cloned.1.call-done = f32[1536,6144]{1,0:T(8,128)} async-done(((f32[48,6144]{1,0:T(8,128)}), f32[1536,6144]{1,0:T(8,128)}) %all-gather.20.cloned.1.call-update) | async-done | bytes 37748752 | tf_op jit(solution)/shard_map/all_gather | solution.py:87
  980.8 26.7 fusion.117
  1007.5 189.4 %all-gather.22.cloned.1.call-done = f32[6144,1536]{1,0:T(8,128)} async-done(((f32[192,1536]{1,0:T(8,128)}), f32[6144,1536]{1,0:T(8,128)}) %all-gather.22.cloned.1.call-update) | async-done | bytes 37748752 | tf_op jit(solution)/shard_map/all_gather | solution.py:88
  1196.9 38.8 %fusion.118 = f32[48,6144]{1,0:T(8,128)S(1)} fusion(f32[48,1536]{1,0:T(8,128)S(1)} %bitcast.232, f32[6144,1536]{1,0:T(8,128)} %all-gather.22.cloned.1.call-done), kind=kOutput, calls=%fused_computation.183 | convolution fusion | flops 5435817984 | bytes 39223296 | tf_op jit(solution)/shard_map/dot_general | solution.py:27
  1235.7 39.7 %fusion.112 = (f32[1536]{0:T(1024)}, f32[1536]{0:T(1024)}, f32[48]{0:T(128)S(1)}, f32[48,1536]{1,0:T(8,128)S(1)}) fusion(f32[3,16,1536]{2,1,0:T(8,128)S(1)} %get-tuple-element.231, f32[1536]{0:T(1024)S(1)} %get-tuple-element.225, f32[1536,6144]{1,0:T(8,128)} %all-gather.20.cloned.1.call-done, f32[48,6144]{1,0:T(8,128)S(1)} %fusion.117, ...), kind=kOutput, calls=%fused_computation.178 | convolution fusion | flops 5441786880 | bytes 40716480 | tf_op jit(solution)/shard_map/dot_general | solution.py:27
  1418.8 157.3 %while.35 = (s32[]{:T(128)}, f32[6,256,1536]{2,1,0:T(8,128)}, f32[6,1536]{1,0:T(8,128)S(1)}, f32[6,1536]{1,0:T(8,128)S(1)}, f32[6,1536]{1,0:T(8,128)S(1)}, /*ind...) while((s32[]{:T(128)}, f32[6,256,1536]{2,1,0:T(8,128)}, ...), condition=%wide.region_25.26_spmd, body=%wide.region_19.25_spmd.sunk | while | flops 14501013504 | bytes 74041528 | solution.py:59
  1614.1 53.3 %bitcast_add_fusion.2 = f32[1536,1536]{1,0:T(8,128)} fusion(f32[1536,1536,1]{1,0,2:T(8,128)S(1)} %fusion.73, f32[1536,1536]{1,0:T(8,128)} %bitcast.225, f32[1536,1536]{1,0:T(8,128)} %bitcast.221), kind=kOutput, calls=%fused_computation.55 | convolution fusion | flops 43488903168 | bytes 37748736 | tf_op jit(solution)/shard_map/dot_general | solution.py:21
  1667.5 24.1 fusion.71
  1691.7 53.7 %bitcast_add_fusion.1 = f32[1536,1536]{1,0:T(8,128)} fusion(f32[1536,1536,1]{1,0,2:T(8,128)S(1)} %fusion.71, f32[1536,1536]{1,0:T(8,128)} %bitcast.226, f32[1536,1536]{1,0:T(8,128)} %bitcast.219), kind=kOutput, calls=%fused_computation.54 | convolution fusion | flops 43488903168 | bytes 37748736 | tf_op jit(solution)/shard_map/dot_general | solution.py:21
  1758.2 33.9 %fusion.108 = f32[1536,6144]{1,0:T(8,128)} fusion(f32[48,1536]{1,0:T(8,128)S(1)} %bitcast.231, f32[48,6144]{1,0:T(8,128)S(1)} %copy-done.2, f32[48,6144]{1,0:T(8,128)S(1)} %copy-done.4), kind=kOutput, calls=%fused_computation.176 | convolution fusion | flops 5441421312 | bytes 40402944 | tf_op jit(solution)/shard_map/dot_general | solution.py:21
  1793.1 34.0 %fusion.65 = f32[6144,1536]{1,0:T(8,128)} fusion(f32[48,1536]{1,0:T(8,128)S(1)} %bitcast.233, f32[48,6144]{1,0:T(8,128)S(1)} %copy-done.2), kind=kOutput, calls=%fused_computation.105 | convolution fusion | flops 5438177280 | bytes 39223296 | tf_op jit(solution)/shard_map/dot_general | solution.py:21
  1827.9 27.4 fusion.66
  1899.2 40.7 %all-reduce.13 = (f32[1536]{0:T(1024)S(1)}, f32[1536]{0:T(1024)S(1)}, f32[1536]{0:T(1024)S(1)}, f32[1536]{0:T(1024)S(1)}, f32[1536]{0:T(1024)S(1)}, /*index=5*/f32[1536]{0:T(1024)S(1)}) all-reduce(f32[1536]{0:T(1024)S(1)} %reduce_sum.217, f32[1536]{0:T(1024)S(1)} %reduce_sum.218, ...), channel_id=9, replica_groups=mesh['seq'=8,'frame'=4] {'seq','frame'}, use_global_device_ids=true, to_apply=%region_33.34.clone | all-reduce | flops 9216 | bytes 73728
  1957.2 141.9 %reduce-scatter.17.cloned.1.call-done = f32[48,1536]{1,0:T(8,128)} async-done(((f32[1536,1536]{1,0:T(8,128)}), f32[48,1536]{1,0:T(8,128)}) %reduce-scatter.17.cloned.1.call-update) | async-done | bytes 294928 | tf_op jit(solution)/shard_map/reduce_scatter | solution.py:313
  2099.1 141.1 %reduce-scatter.13.cloned.1.call-done = f32[48,1536]{1,0:T(8,128)} async-done(((f32[1536,1536]{1,0:T(8,128)}), f32[48,1536]{1,0:T(8,128)}) %reduce-scatter.13.cloned.1.call-update) | async-done | bytes 294928 | tf_op jit(solution)/shard_map/reduce_scatter | solution.py:311
  2240.2 355.5 %reduce-scatter.21.cloned.1.call-done = f32[48,6144]{1,0:T(8,128)} async-done(((f32[1536,6144]{1,0:T(8,128)}), f32[48,6144]{1,0:T(8,128)}) %reduce-scatter.21.cloned.1.call-update) | async-done | bytes 1179664 | tf_op jit(solution)/shard_map/reduce_scatter | solution.py:315
  2595.7 354.7 %reduce-scatter.23.cloned.1.call-done = f32[192,1536]{1,0:T(8,128)} async-done(((f32[6144,1536]{1,0:T(8,128)}), f32[192,1536]{1,0:T(8,128)}) %reduce-scatter.23.cloned.1.call-update) | async-done | bytes 1179664 | tf_op jit(solution)/shard_map/reduce_scatter | solution.py:316
  (424 shorter events, 828.9 us)
Async XLA Ops:
  7.2 92.8 %all-gather.10.cloned.1.call-start = ((), (), s32[]{:S(2)}) async-start(), calls=%async_computation.8 | async-start | bytes 1474560 | tf_op jit(solution)/shard_map/all_gather | solution.py:122
  7.9 108.6 %all-gather.16.cloned.1.call-start = ((), (), s32[]{:S(2)}) async-start(), calls=%async_computation.11 | async-start | bytes 9732096 | tf_op jit(solution)/shard_map/all_gather | solution.py:83
  8.7 191.4 %all-gather.14.cloned.1.call-start = ((), (), s32[]{:S(2)}) async-start(), calls=%async_computation.10 | async-start | bytes 9732096 | tf_op jit(solution)/shard_map/all_gather | solution.py:84
  9.4 274.1 %all-gather.12.cloned.1.call-start = ((), (), s32[]{:S(2)}) async-start(), calls=%async_computation.9 | async-start | bytes 9732096 | tf_op jit(solution)/shard_map/all_gather | solution.py:85
  10.0 669.4 %all-reduce.17.cloned.1.call-start = ((), (), s32[]{:S(2)}) async-start(), calls=%async_computation.12 | async-start | bytes 3145728 | tf_op jit(solution)/shard_map/psum | solution.py:190
  103.3 497.7 %copy-start.12 = (f32[3,64,1536]{2,1,0:T(8,128)}, f32[3,64,1536]{2,1,0:T(8,128)S(1)}, u32[]{:S(2)}) copy-start(f32[3,64,1536]{2,1,0:T(8,128)S(1)} %get-tuple-element.232) | copy-start | bytes 3538948
  637.4 126.9 %all-gather.18.cloned.1.call-start = ((), (), s32[]{:S(2)}) async-start(), calls=%async_computation.13 | async-start | bytes 9732096 | tf_op jit(solution)/shard_map/all_gather | solution.py:86
  638.0 342.8 %all-gather.20.cloned.1.call-start = ((), (), s32[]{:S(2)}) async-start(), calls=%async_computation.14 | async-start | bytes 38928384 | tf_op jit(solution)/shard_map/all_gather | solution.py:87
  638.7 558.1 %all-gather.22.cloned.1.call-start = ((), (), s32[]{:S(2)}) async-start(), calls=%async_computation.15 | async-start | bytes 38928384 | tf_op jit(solution)/shard_map/all_gather | solution.py:88
  639.5 664.0 %all-gather.24.cloned.1.call-start = ((), (), s32[]{:S(2)}) async-start(), calls=%async_computation.16 | async-start | bytes 1474560 | tf_op jit(solution)/shard_map/all_gather | solution.py:239
  682.2 82.1 %copy-start.21 = (f32[3,16,1536]{2,1,0:T(8,128)S(1)}, f32[3,16,1536]{2,1,0:T(8,128)}, u32[]{:S(2)}) copy-start(f32[3,16,1536]{2,1,0:T(8,128)} %param.22) | copy-start | bytes 884740
  683.0 89.6 %copy-start.20 = (f32[3,64,1536]{2,1,0:T(8,128)}, f32[3,64,1536]{2,1,0:T(8,128)S(1)}, u32[]{:S(2)}) copy-start(f32[3,64,1536]{2,1,0:T(8,128)S(1)} %reshape.338) | copy-start | bytes 3538948
  773.4 234.1 %copy-start.16 = (f32[3,16,1536]{2,1,0:T(8,128)}, f32[3,16,1536]{2,1,0:T(8,128)S(1)}, u32[]{:S(2)}) copy-start(f32[3,16,1536]{2,1,0:T(8,128)S(1)} %get-tuple-element.230) | copy-start | bytes 884740
  980.8 216.1 %copy-start.18 = (f32[3,16,1536]{2,1,0:T(8,128)S(1)}, f32[3,16,1536]{2,1,0:T(8,128)}, u32[]{:S(2)}) copy-start(f32[3,16,1536]{2,1,0:T(8,128)} %param.39) | copy-start | bytes 884740
  1007.5 228.2 %copy-start.1 = (f32[48,6144]{1,0:T(8,128)}, f32[48,6144]{1,0:T(8,128)S(1)}, u32[]{:S(2)}) copy-start(f32[48,6144]{1,0:T(8,128)S(1)} %fusion.117) | copy-start | bytes 3538948
  1287.7 457.8 %reduce-scatter.11.cloned.1.call-start = ((), (), s32[]{:S(2)}) async-start(), calls=%async_computation.17 | async-start | bytes 1474560 | tf_op jit(solution)/shard_map/reduce_scatter | solution.py:270
  1373.3 491.1 %reduce-scatter.25.cloned.1.call-start = ((), (), s32[]{:S(2)}) async-start(), calls=%async_computation.24 | async-start | bytes 811008
  1418.8 157.3 %copy-start.30 = (s32[6]{0:T(128)S(1)}, s32[6]{0:T(128)}, u32[]{:S(2)}) copy-start(s32[6]{0:T(128)} %copy-done.29) | copy-start | bytes 76
  1577.8 366.4 %reduce-scatter.19.cloned.1.call-start = ((), (), s32[]{:S(2)}) async-start(), calls=%async_computation.21 | async-start | bytes 9732096 | tf_op jit(solution)/shard_map/reduce_scatter | solution.py:314
  1588.8 368.5 %reduce-scatter.15.cloned.1.call-start = ((), (), s32[]{:S(2)}) async-start(), calls=%async_computation.19 | async-start | bytes 9732096 | tf_op jit(solution)/shard_map/reduce_scatter | solution.py:312
  1667.5 431.6 %reduce-scatter.17.cloned.1.call-start = ((), (), s32[]{:S(2)}) async-start(), calls=%async_computation.20 | async-start | bytes 9732096 | tf_op jit(solution)/shard_map/reduce_scatter | solution.py:313
  1745.4 494.8 %reduce-scatter.13.cloned.1.call-start = ((), (), s32[]{:S(2)}) async-start(), calls=%async_computation.18 | async-start | bytes 9732096 | tf_op jit(solution)/shard_map/reduce_scatter | solution.py:311
  1756.5 839.2 %reduce-scatter.21.cloned.1.call-start = ((), (), s32[]{:S(2)}) async-start(), calls=%async_computation.22 | async-start | bytes 38928384 | tf_op jit(solution)/shard_map/reduce_scatter | solution.py:315
  1792.2 1158.2 %reduce-scatter.23.cloned.1.call-start = ((), (), s32[]{:S(2)}) async-start(), calls=%async_computation.23 | async-start | bytes 38928384 | tf_op jit(solution)/shard_map/reduce_scatter | solution.py:316
  (63 other events, 972.9 us)
Sparse Core Ops, SparseCore 0:
  9.6 20.4 all-gather.9
  33.0 83.4 all-gather.15
  119.4 80.6 all-gather.13
  202.8 80.6 all-gather.11
  637.5 41.8 all-reduce.16
  682.1 82.0 all-gather.17
  767.2 213.6 all-gather.19
  983.7 213.1 all-gather.21
  1287.8 15.6 all-gather.23
  1373.4 25.7 reduce-scatter.10
  1578.0 95.5 reduce-scatter.24
  1680.9 134.4 reduce-scatter.18
  1821.9 135.2 reduce-scatter.14
  1964.5 134.5 reduce-scatter.16
  2105.4 134.7 reduce-scatter.12
  2248.2 347.4 reduce-scatter.20
  2602.6 347.8 reduce-scatter.22
where the time goes:
time: 2970 us; the launch traced here: 2960 us
  waiting for transfers between devices  1700 us (57%)
  matrix products  847 us (29%)
  local copies, waits for them, and re-layouts  172 us (6%)
  blocking collectives  147 us (5%)
  other arithmetic  70.8 us (2%)
    reduce_scatter x1, waiting for transfers between devices, body(): lax.psum_scatter(grad_up, ('seq', 'frame'), scatter_dimension=0, tiled=True)  356 us
    reduce_scatter x1, waiting for transfers between devices, body(): lax.psum_scatter(grad_down, ('seq', 'frame'), scatter_dimension=0, tiled=...  355 us
    dot_general x18, matrix products, product_nt(): lax.dot_general(left, right, (((1,), (1,)), ((), ())), precision=HIGHEST,...  253 us
    dot_general x8, matrix products, product_tn(): lax.dot_general(left, right, (((0,), (0,)), ((), ())), precision=HIGHEST,...  245 us
    dot_general x17, matrix products, product(): jnp.dot(left, right, precision=HIGHEST, preferred_element_type=jnp.float32)  217 us
    all_gather x1, waiting for transfers between devices, body(): lax.all_gather(up_proj, ('seq', 'frame'), axis=0, tiled=True)  207 us
    all_gather x1, waiting for transfers between devices, body(): lax.all_gather(down_proj, ('seq', 'frame'), axis=0, tiled=True)  189 us
    reduce_scatter x1, waiting for transfers between devices, body(): lax.psum_scatter(grad_value_w, ('seq', 'frame'), scatter_dimension=0, til...  142 us
  transfers between devices with their start and end apart: 17, of which 13 were waited for; matrix products, arithmetic and copies ran while one was open for 20% of the time, Pallas kernels for 0%

commit v1 on v0

--- a/solution.py
+++ b/solution.py
@@ -1,8 +1,11 @@
+import functools
 import math
 
 import jax
 import jax.numpy as jnp
 from jax import lax
+from jax.experimental import pallas as pl
+from jax.experimental.pallas import tpu as pltpu
 from jax.sharding import PartitionSpec as P
 
 HEADS = 16
@@ -59,7 +62,7 @@
     return lax.map(action, operands)
 
 
-def body(
+def body_general(
     latents,
     patch_feats,
     image_counts,
@@ -94,6 +97,7 @@
         lax.all_gather(feed_bias, ("seq", "frame"), axis=0, tiled=True),
         lax.all_gather(time_table, ("seq", "frame"), axis=1, tiled=True),
     )
+    gathered = lax.optimization_barrier(gathered)
     (
         query_full,
         key_full,
@@ -214,6 +218,7 @@
         lax.all_gather(feed_bias, ("seq", "frame"), axis=0, tiled=True),
         lax.all_gather(time_table, ("seq", "frame"), axis=1, tiled=True),
     )
+    regathered = lax.optimization_barrier(regathered)
     query_back = regathered[0]
     key_back = regathered[1]
     value_back = regathered[2]
@@ -307,6 +312,16 @@
     grad_mbias = jnp.sum(bias_parts, axis=0)
     grad_table = product_tn(one_hot, slot_sums)
     patch_grads = feats_grads.reshape(patch_feats.shape)
+    (
+        grad_query_w,
+        grad_key_w,
+        grad_value_w,
+        grad_out_w,
+        grad_up,
+        grad_down,
+    ) = lax.optimization_barrier(
+        (grad_query_w, grad_key_w, grad_value_w, grad_out_w, grad_up, grad_down)
+    )
     summed = (
         lax.psum_scatter(grad_query_w, ("seq", "frame"), scatter_dimension=0, tiled=True),
         lax.psum_scatter(grad_key_w, ("seq", "frame"), scatter_dimension=0, tiled=True),
@@ -342,9 +357,1206 @@
     )
 
 
+MESH = pl.DeviceIdType.MESH
+F32 = jnp.float32
+ANY = pl.BlockSpec(memory_space=pl.ANY)
+GRID = (4, 2, 2, 2)
+
+
+def place(z, y, x, c):
+    return (z * 2 + y, x * 2 + c)
+
+
+class Here:
+    def __init__(self):
+        seq, frame = lax.axis_index("seq"), lax.axis_index("frame")
+        self.z, self.y, self.x, self.c = z, y, x, c = seq // 2, seq % 2, frame // 2, frame % 2
+        self.ox, self.oy, self.oc = ox, oy, oc = 1 - x, 1 - y, 1 - c
+        self.at_x, self.at_y, self.at_c = place(z, y, ox, c), place(z, oy, x, c), place(z, y, x, oc)
+        self.ahead = [lax.rem(z + k, 4) for k in range(4)]
+        self.behind = [lax.rem(z + 4 - k, 4) for k in range(4)]
+        self.at_z = [place(o, y, x, c) for o in self.ahead]
+
+    def greet(self):
+        barrier = pltpu.get_barrier_semaphore()
+        for peer in self.at_z[1:] + [self.at_x, self.at_y, self.at_c]:
+            pl.semaphore_signal(barrier, inc=1, device_id=peer, device_id_type=MESH)
+        pl.semaphore_wait(barrier, 6)
+
+
+def remote(src, dst, send_sem, recv_sem, peer):
+    return pltpu.make_async_remote_copy(
+        src_ref=src, dst_ref=dst, send_sem=send_sem, recv_sem=recv_sem, device_id=peer, device_id_type=MESH
+    )
+
+
+class Gather:
+    def __init__(self, here, shards, fulls, cuts, sems):
+        self.here, self.count = here, len(cuts)
+        self.loc, self.zs, self.zr, self.xs, self.xr, self.ys, self.yr, self.ds, self.dr, self.cs, self.cr = sems
+        self.shard = [shards[a].at[:, lo:hi] for a, lo, hi in cuts]
+        self.full = [(lambda *at, a=a, lo=lo, hi=hi: fulls[a].at[at + (slice(lo, hi),)]) for a, lo, hi in cuts]
+        self.half = [shards[a].shape[0] // 2 for a, lo, hi in cuts]
+
+    @staticmethod
+    def semaphores(count):
+        dma = pltpu.SemaphoreType.DMA
+        shapes = [(), (3,), (3,), (4,), (4,), (4,), (4,), (2, 4), (2, 4), (4,), (4,)]
+        return [dma((count,) + s) for s in shapes]
+
+    def local(self, p):
+        h = self.here
+        return pltpu.make_async_copy(self.shard[p], self.full[p](h.z, h.y, h.x, h.c, slice(None)), self.loc.at[p])
+
+    def over_z(self, p, k):
+        h = self.here
+        dst = self.full[p](h.z, h.y, h.x, h.c, slice(None))
+        return remote(self.shard[p], dst, self.zs.at[p, k - 1], self.zr.at[p, k - 1], h.at_z[k])
+
+    def over_x(self, p, k):
+        h = self.here
+        block = self.full[p](h.behind[k], h.y, h.x, h.c, slice(None))
+        return remote(self.shard[p] if k == 0 else block, block, self.xs.at[p, k], self.xr.at[p, k], h.at_x)
+
+    def over_y(self, p, k):
+        h = self.here
+        block = self.full[p](h.behind[k], h.y, h.x, h.c, slice(None))
+        return remote(self.shard[p] if k == 0 else block, block, self.ys.at[p, k], self.yr.at[p, k], h.at_y)
+
+    def on_y(self, p, k):
+        h = self.here
+        part = self.full[p](h.behind[k], h.y, h.ox, h.c, slice(self.half[p], 2 * self.half[p]))
+        return remote(part, part, self.ds.at[p, 0, k], self.dr.at[p, 0, k], h.at_y)
+
+    def on_x(self, p, k):
+        h = self.here
+        part = self.full[p](h.behind[k], h.oy, h.x, h.c, slice(0, self.half[p]))
+        return remote(part, part, self.ds.at[p, 1, k], self.dr.at[p, 1, k], h.at_x)
+
+    def to_core(self, p, i):
+        h = self.here
+        yy, xx = ((h.y, h.x), (h.y, h.ox), (h.oy, h.x), (h.oy, h.ox))[i]
+        blocks = self.full[p](slice(None), yy, xx, h.c, slice(None))
+        return remote(blocks, blocks, self.cs.at[p, i], self.cr.at[p, i], h.at_c)
+
+    def own(self, p):
+        self.local(p).start()
+        for k in (1, 2, 3):
+            self.over_z(p, k).start()
+        self.over_x(p, 0).start()
+        self.over_y(p, 0).start()
+
+    def along_z(self, p):
+        for k in (1, 2, 3):
+            self.over_z(p, k).wait_recv()
+            self.over_x(p, k).start()
+            self.over_y(p, k).start()
+
+    def across(self, p):
+        for k in range(4):
+            self.over_x(p, k).wait_recv()
+            self.on_y(p, k).start()
+            self.over_y(p, k).wait_recv()
+            self.on_x(p, k).start()
+        self.local(p).wait()
+        for i in range(3):
+            self.to_core(p, i).start()
+
+    def corner(self, p):
+        for k in range(4):
+            self.on_y(p, k).wait_recv()
+            self.on_x(p, k).wait_recv()
+        self.to_core(p, 3).start()
+
+    def done(self, p):
+        for i in range(4):
+            self.to_core(p, i).wait()
+        for k in (1, 2, 3):
+            self.over_z(p, k).wait_send()
+        for k in range(4):
+            for copy in (self.over_x, self.over_y, self.on_x, self.on_y):
+                copy(p, k).wait_send()
+
+    def stages(self):
+        return (self.own, self.along_z, self.across, self.corner)
+
+
+LAG = 2
+
+
+def waves_of(plan):
+    stages = plan.stages()
+    order = [0] + list(range(len(stages) - 1, 0, -1))
+    return [
+        [functools.partial(stages[s], t - s * LAG) for s in order if 0 <= t - s * LAG < plan.count]
+        for t in range(plan.count + (len(stages) - 1) * LAG)
+    ]
+
+
+def finish_all(plan):
+    for p in range(plan.count):
+        plan.done(p)
+
+
+class Scatter:
+    def __init__(self, here, count, mine, theirs, load, out, scratch):
+        self.here, self.count, self.mine, self.theirs, self.load, self.out = here, count, mine, theirs, load, out
+        self.got, self.gx, self.gy, self.hx, self.hy, self.gz = scratch[:6]
+        self.cs, self.cr, self.fs, self.fr, self.ss, self.sr, self.zs, self.zr = scratch[6:]
+        self.half = self.got.shape[-2] // 2
+
+    @staticmethod
+    def scratch(count, r, w):
+        dma = pltpu.SemaphoreType.DMA
+        leads = [(4, 2, 2, r), (4, 2, r // 2), (4, 2, r // 2), (4, r // 2), (4, r // 2), (3, r)]
+        return [pltpu.VMEM((count,) + s + (w,), F32) for s in leads] + [
+            dma((count,) + s) for s in ((), (), (2,), (2,), (2,), (2,), (3,), (3,))
+        ]
+
+    def to_core(self, p):
+        return remote(self.theirs(p), self.got.at[p], self.cs.at[p], self.cr.at[p], self.here.at_c)
+
+    def first(self, p, way):
+        h, half, tot = self.here, self.half, self.mine(p)
+        if way == 0:
+            return remote(tot.at[:, :, h.ox, :half], self.gx.at[p], self.fs.at[p, 0], self.fr.at[p, 0], h.at_x)
+        return remote(tot.at[:, h.oy, :, half:], self.gy.at[p], self.fs.at[p, 1], self.fr.at[p, 1], h.at_y)
+
+    def second(self, p, way):
+        h, half, tot = self.here, self.half, self.mine(p)
+        if way == 0:
+            return remote(tot.at[:, h.oy, h.x, :half], self.hy.at[p], self.ss.at[p, 0], self.sr.at[p, 0], h.at_y)
+        return remote(tot.at[:, h.y, h.ox, half:], self.hx.at[p], self.ss.at[p, 1], self.sr.at[p, 1], h.at_x)
+
+    def over_z(self, p, k):
+        h = self.here
+        src = self.mine(p).at[h.ahead[k], h.y, h.x]
+        return remote(src, self.gz.at[p, k - 1], self.zs.at[p, k - 1], self.zr.at[p, k - 1], h.at_z[k])
+
+    def start(self, p):
+        if self.load is not None:
+            self.load(p).start()
+        self.to_core(p).start()
+
+    def cores(self, p):
+        tot, got = self.mine(p), self.got.at[p]
+        if self.load is not None:
+            self.load(p).wait()
+        self.to_core(p).wait_recv()
+
+        @pl.loop(0, 16)
+        def _(i):
+            at = (i // 4, (i // 2) % 2, i % 2)
+            tot[at] = tot[at] + got[at]
+
+        self.first(p, 0).start()
+        self.first(p, 1).start()
+
+    def sides(self, p):
+        h, half, tot = self.here, self.half, self.mine(p)
+        gx, gy = self.gx.at[p], self.gy.at[p]
+        self.first(p, 0).wait_recv()
+
+        @pl.loop(0, 8)
+        def _(i):
+            zi, yi = i // 2, i % 2
+            tot[zi, yi, h.x, :half] = tot[zi, yi, h.x, :half] + gx[zi, yi]
+
+        self.second(p, 0).start()
+        self.first(p, 1).wait_recv()
+
+        @pl.loop(0, 8)
+        def _(i):
+            zi, xi = i // 2, i % 2
+            tot[zi, h.y, xi, half:] = tot[zi, h.y, xi, half:] + gy[zi, xi]
+
+        self.second(p, 1).start()
+
+    def column(self, p):
+        h, half, tot = self.here, self.half, self.mine(p)
+        hx, hy = self.hx.at[p], self.hy.at[p]
+        self.second(p, 0).wait_recv()
+        self.second(p, 1).wait_recv()
+
+        @pl.loop(0, 4)
+        def _(zi):
+            tot[zi, h.y, h.x, :half] = tot[zi, h.y, h.x, :half] + hy[zi]
+            tot[zi, h.y, h.x, half:] = tot[zi, h.y, h.x, half:] + hx[zi]
+
+        for k in (1, 2, 3):
+            self.over_z(p, k).start()
+
+    def finish(self, p):
+        h, gz = self.here, self.gz.at[p]
+        for k in (1, 2, 3):
+            self.over_z(p, k).wait_recv()
+        self.out(p)[...] = (self.mine(p)[h.z, h.y, h.x] + gz[0]) + (gz[1] + gz[2])
+
+    def done(self, p):
+        self.to_core(p).wait_send()
+        for way in (0, 1):
+            self.first(p, way).wait_send()
+            self.second(p, way).wait_send()
+        for k in (1, 2, 3):
+            self.over_z(p, k).wait_send()
+
+    def stages(self):
+        return (self.start, self.cores, self.sides, self.column, self.finish)
+
+
+def run(wave):
+    for action in wave:
+        action()
+
+
+def run_tick(step, steps, part, parts, waves):
+    ticks, total, before, starts = steps * parts, sum(len(w) for w in waves), 0, []
+    for wave in waves:
+        starts.append(ticks * before // total)
+        before += len(wave)
+    for tick in range(part, ticks, parts):
+        now = [wave for wave, start in zip(waves, starts) if start == tick]
+        if now:
+
+            @pl.when(step == tick // parts)
+            def _():
+                for wave in now:
+                    run(wave)
+
+
+def run_last(step, steps, plan):
+    @pl.when(step == steps - 1)
+    def _():
+        finish_all(plan)
+
+
+def column_cuts(widths, pieces):
+    return [(a, w * i // n, w * (i + 1) // n) for a, (w, n) in enumerate(zip(widths, pieces)) for i in range(n)]
+
+
+class GroupGather:
+    def __init__(self, here, shards, fulls, sems):
+        self.here, self.shards, self.fulls, self.count = here, shards, fulls, len(shards)
+        self.loc, self.ss, self.rs = sems
+
+    @staticmethod
+    def semaphores(count):
+        dma = pltpu.SemaphoreType.DMA
+        return [dma((count,)), dma((count, 3)), dma((count, 3))]
+
+    def local(self, a):
+        h = self.here
+        return pltpu.make_async_copy(self.shards[a], self.fulls[a].at[:, h.x * 2 + h.c], self.loc.at[a])
+
+    def copy(self, a, i):
+        h = self.here
+        mine = self.fulls[a].at[:, h.x * 2 + h.c]
+        if i < 2:
+            return remote(self.shards[a], mine, self.ss.at[a, i], self.rs.at[a, i], (h.at_x, h.at_c)[i])
+        block = self.fulls[a].at[:, h.ox * 2 + h.c]
+        return remote(block, block, self.ss.at[a, 2], self.rs.at[a, 2], h.at_c)
+
+    def start(self):
+        for a in range(self.count):
+            self.local(a).start()
+            self.copy(a, 0).start()
+            self.copy(a, 1).start()
+
+    def forward(self):
+        for a in range(self.count):
+            self.copy(a, 0).wait_recv()
+            self.copy(a, 2).start()
+
+    def done(self):
+        for a in range(self.count):
+            self.local(a).wait()
+            self.copy(a, 0).wait_send()
+            self.copy(a, 1).wait()
+            self.copy(a, 2).wait()
+
+
+def first_kernel(count, cuts, *refs):
+    here = Here()
+    group = GroupGather(here, refs[count : count + 1], refs[2 * count + 1 : 2 * count + 2], refs[-3:])
+    plan = Gather(here, refs[:count], refs[count + 1 : 2 * count + 1], cuts, refs[2 * count + 2 : -3])
+    waves = waves_of(plan)
+    waves[0] = [here.greet, group.start] + waves[0]
+    waves[3].append(group.forward)
+    for wave in waves:
+        run(wave)
+    group.done()
+    finish_all(plan)
+
+
+def gather_first(shards, pieces, rows, collective_id):
+    count = len(shards)
+    cuts = column_cuts([s.shape[1] for s in shards], pieces)
+    s, r, w = rows.shape
+    *outs, group = pl.pallas_call(
+        functools.partial(first_kernel, count, cuts),
+        out_shape=full_shapes(shards) + [jax.ShapeDtypeStruct((s, 4, r, w), F32)],
+        in_specs=[ANY] * (count + 1),
+        out_specs=[ANY] * (count + 1),
+        scratch_shapes=Gather.semaphores(len(cuts)) + GroupGather.semaphores(1),
+        compiler_params=pltpu.CompilerParams(collective_id=collective_id, has_side_effects=True),
+        name="gather_first",
+    )(*shards, rows)
+    return [flat_full(o) for o in outs], group
+
+
+def flat_full(full):
+    return full.reshape((-1, full.shape[-1]))
+
+
+def full_shapes(shards):
+    return [jax.ShapeDtypeStruct(GRID + s.shape, s.dtype) for s in shards]
+
+
+def gather_kernel(count, cuts, *refs):
+    here = Here()
+    here.greet()
+    plan = Gather(here, refs[:count], refs[count : 2 * count], cuts, refs[2 * count :])
+    for wave in waves_of(plan):
+        run(wave)
+    finish_all(plan)
+
+
+def gather_all(shards, pieces, collective_id):
+    count = len(shards)
+    cuts = column_cuts([s.shape[1] for s in shards], pieces)
+    outs = pl.pallas_call(
+        functools.partial(gather_kernel, count, cuts),
+        out_shape=full_shapes(shards),
+        in_specs=[ANY] * count,
+        out_specs=[ANY] * count,
+        scratch_shapes=Gather.semaphores(len(cuts)),
+        compiler_params=pltpu.CompilerParams(collective_id=collective_id, has_side_effects=True),
+        name="gather_all",
+    )(*shards)
+    return [flat_full(o) for o in outs]
+
+
+class Summed:
+    def __init__(self, parts, pieces):
+        self.arrays, self.pieces = len(parts), pieces
+        self.rows, self.width = parts[0].shape[0] // 32, parts[0].shape[1]
+        self.cut = self.width // pieces
+        self.operands = [p.reshape(GRID + (self.rows, self.width)) for p in parts]
+        self.in_specs = [ANY] * len(parts)
+        self.out_shape = [jax.ShapeDtypeStruct((self.rows, self.width), F32)] * len(parts)
+        self.out_specs = [whole((self.rows, self.width))] * len(parts)
+        n = self.count = len(parts) * pieces
+        self.scratch = [pltpu.VMEM((n, 4, 2, 2, self.rows, self.cut), F32), pltpu.SemaphoreType.DMA((n,))]
+        self.scratch += Scatter.scratch(n, self.rows, self.cut)
+
+    def bind(self, here, ins, outs, scratch):
+        tots, loc = scratch[:2]
+
+        def cut(p):
+            return p // self.pieces, pl.ds(p % self.pieces * self.cut, self.cut)
+
+        def part(p, core):
+            a, cols = cut(p)
+            return ins[a].at[:, :, :, core, :, cols]
+
+        def out(p):
+            a, cols = cut(p)
+            return outs[a].at[:, cols]
+
+        return Scatter(
+            here,
+            self.count,
+            lambda p: tots.at[p],
+            lambda p: part(p, here.oc),
+            lambda p: pltpu.make_async_copy(part(p, here.c), tots.at[p], loc.at[p]),
+            out,
+            scratch[2:],
+        )
+
+
+def scatter_kernel(plan, *refs):
+    n = plan.arrays
+    here = Here()
+    here.greet()
+    sums = plan.bind(here, refs[:n], refs[n : 2 * n], refs[2 * n :])
+    for wave in waves_of(sums):
+        run(wave)
+    finish_all(sums)
+
+
+def scatter_all(parts, pieces, collective_id):
+    plan = Summed(parts, pieces)
+    return pl.pallas_call(
+        functools.partial(scatter_kernel, plan),
+        out_shape=plan.out_shape,
+        in_specs=plan.in_specs,
+        out_specs=[pl.BlockSpec(memory_space=pltpu.VMEM)] * len(parts),
+        scratch_shapes=plan.scratch,
+        compiler_params=pltpu.CompilerParams(
+            collective_id=collective_id, has_side_effects=True, vmem_limit_bytes=60 * 2**20
+        ),
+        name="scatter_all",
+    )(*plan.operands)
+
+
+def greet(peers):
+    barrier = pltpu.get_barrier_semaphore()
+    for peer in peers:
+        pl.semaphore_signal(barrier, inc=1, device_id=peer, device_id_type=MESH)
+    pl.semaphore_wait(barrier, len(peers))
+
+
+def group_gather_kernel(count, *refs):
+    shards, fulls = refs[:count], refs[count : 2 * count]
+    loc, ss, rs = refs[2 * count :]
+    here = Here()
+    x, c, ox, at_x, at_c = here.x, here.c, here.ox, here.at_x, here.at_c
+    greet([at_x, at_c])
+    waits = []
+    for a in range(count):
+        mine = fulls[a].at[:, x * 2 + c]
+        copy = pltpu.make_async_copy(shards[a], mine, loc.at[a])
+        copy.start()
+        over = remote(shards[a], mine, ss.at[a, 0], rs.at[a, 0], at_x)
+        over.start()
+        side = remote(shards[a], mine, ss.at[a, 1], rs.at[a, 1], at_c)
+        side.start()
+        waits.append((copy, over, side))
+    last = []
+    for a in range(count):
+        waits[a][1].wait_recv()
+        block = fulls[a].at[:, ox * 2 + c]
+        on = remote(block, block, ss.at[a, 2], rs.at[a, 2], at_c)
+        on.start()
+        last.append(on)
+    for a in range(count):
+        copy, over, side = waits[a]
+        copy.wait()
+        over.wait_send()
+        side.wait()
+        last[a].wait()
+
+
+def group_gather(shards, collective_id):
+    count = len(shards)
+    dma = pltpu.SemaphoreType.DMA
+    return pl.pallas_call(
+        functools.partial(group_gather_kernel, count),
+        out_shape=[jax.ShapeDtypeStruct((s.shape[0], 4) + s.shape[1:], F32) for s in shards],
+        in_specs=[ANY] * count,
+        out_specs=[ANY] * count,
+        scratch_shapes=[dma((count,)), dma((count, 3)), dma((count, 3))],
+        compiler_params=pltpu.CompilerParams(collective_id=collective_id, has_side_effects=True),
+        name="group_gather",
+    )(*shards)
+
+
+def group_swap_kernel(count, *refs):
+    shards, fulls = refs[:count], refs[count : 2 * count]
+    loc, ss, rs = refs[2 * count :]
+    here = Here()
+    z, y, x, c = here.z, here.y, here.x, here.c
+    me = x * 2 + c
+    peers = [(x, 1 - c), (1 - x, c), (1 - x, 1 - c)]
+    greet([place(z, y, *p) for p in peers])
+    waits = []
+    for a in range(count):
+        copy = pltpu.make_async_copy(shards[a].at[:, me], fulls[a].at[:, me], loc.at[a])
+        copy.start()
+        waits.append(copy)
+        for k in (1, 2, 0):
+            px, pc = peers[k]
+            on = remote(
+                shards[a].at[:, px * 2 + pc], fulls[a].at[:, me], ss.at[a, k], rs.at[a, k], place(z, y, px, pc)
+            )
+            on.start()
+            waits.append(on)
+    for copy in waits:
+        copy.wait()
+
+
+def group_swap(shards, collective_id):
+    count = len(shards)
+    dma = pltpu.SemaphoreType.DMA
+    return pl.pallas_call(
+        functools.partial(group_swap_kernel, count),
+        out_shape=[jax.ShapeDtypeStruct(s.shape, F32) for s in shards],
+        in_specs=[ANY] * count,
+        out_specs=[ANY] * count,
+        scratch_shapes=[dma((count,)), dma((count, 3)), dma((count, 3))],
+        compiler_params=pltpu.CompilerParams(collective_id=collective_id, has_side_effects=True),
+        name="group_swap",
+    )(*shards)
+
+
+BF16 = jnp.bfloat16
+HIGH = lax.Precision.HIGH
+BLOCK = 256
+
+
+def dot(left, right, dims=(1, 0)):
+    return lax.dot_general(
+        left, right, (((dims[0],), (dims[1],)), ((), ())), precision=HIGH, preferred_element_type=F32
+    )
+
+
+def dot3(left, right, dims=(1, 0)):
+    numbers = (((dims[0],), (dims[1],)), ((), ()))
+    one = functools.partial(lax.dot_general, dimension_numbers=numbers, preferred_element_type=F32)
+    return one(left[0], right[0]) + (one(left[0], right[1]) + one(left[1], right[0]))
+
+
+def halves(values):
+    top = values.astype(BF16)
+    return top, (values - top.astype(F32)).astype(BF16)
+
+
+def split_weights(sources, pairs, stage, sems):
+    step = stage.shape[1]
+    chunks = [(i, r) for i, s in enumerate(sources) for r in range(0, s.shape[0], step)]
+
+    def copy(n):
+        i, r = chunks[n]
+        return pltpu.make_async_copy(sources[i].at[r : r + step], stage.at[n % 2], sems.at[n % 2])
+
+    copy(0).start()
+    for n, (i, r) in enumerate(chunks):
+        if n + 1 < len(chunks):
+            copy(n + 1).start()
+        copy(n).wait()
+        pairs[i][0][r : r + step], pairs[i][1][r : r + step] = halves(stage[n % 2])
+
+
+def unit_of(values):
+    centred = values - jnp.mean(values, axis=-1, keepdims=True)
+    inv_std = lax.rsqrt(jnp.mean(centred * centred, axis=-1, keepdims=True) + EPSILON)
+    return centred * inv_std, inv_std
+
+
+def staging(width):
+    return [pltpu.VMEM((width, width), BF16)] * 4 + [pltpu.VMEM((2, 128, width), F32), pltpu.SemaphoreType.DMA((2,))]
+
+
+def media_kernel(cuts, steps, *refs):
+    feats, embed, gain, bias, own, key_w, value_w = refs[:7]
+    n = max(a for a, _, _ in cuts) + 1
+    shards, outs = refs[7 : 7 + n], refs[7 + n :]
+    keys, values, own_keys, own_values, xt_top, xt_low = outs[:6]
+    fulls, (kt, kl, vt, vl, stage, sems), rest = outs[6 : 6 + n], outs[6 + n : 12 + n], outs[12 + n :]
+    step = pl.program_id(0)
+    here = Here()
+    moved = Gather(here, shards, fulls, cuts, rest)
+    waves = waves_of(moved)
+    waves[0].insert(0, here.greet)
+
+    @pl.when(step == 0)
+    def _():
+        split_weights((key_w, value_w), ((kt, kl), (vt, vl)), stage, sems)
+        mine = halves(own[...])
+        own_keys[...] = dot3(mine, (kt[...], kl[...]))
+        own_values[...] = dot3(mine, (vt[...], vl[...]))
+
+    unit, _ = unit_of(feats[...] + embed[...])
+    normed = unit * gain[...] + bias[...]
+    flipped = halves(jnp.swapaxes(normed, 0, 1))
+    xt_top[...], xt_low[...] = flipped
+    pair = halves(normed)
+    for i in range(6):
+        run_tick(step, steps, i, 6, waves)
+        cols = slice(i % 3 * 512, i % 3 * 512 + 512)
+        if i < 3:
+            keys[:, cols] = dot3(pair, (kt[:, cols], kl[:, cols]))
+        else:
+            values[:, cols] = dot3(pair, (vt[:, cols], vl[:, cols]))
+    run_last(step, steps, moved)
+
+
+def whole(shape, buffers=1):
+    return pl.BlockSpec(shape, lambda *i: (0,) * len(shape), pipeline_mode=pl.Buffered(buffers))
+
+
+def media_forward(feats, embed, gain, bias, own, key_w, value_w, shards, pieces, collective_id):
+    rows, width = feats.shape
+    own_rows = own.shape[0]
+    cuts = column_cuts([s.shape[1] for s in shards], pieces)
+    row_block = pl.BlockSpec((BLOCK, width), lambda i: (i, 0))
+    full = jax.ShapeDtypeStruct((rows, width), F32)
+    small = jax.ShapeDtypeStruct((own_rows, width), F32)
+    turned = jax.ShapeDtypeStruct((width, rows), BF16)
+    turned_block = pl.BlockSpec((width, BLOCK), lambda i: (0, i))
+    outs = pl.pallas_call(
+        functools.partial(media_kernel, cuts, rows // BLOCK),
+        grid=(rows // BLOCK,),
+        in_specs=[
+            row_block,
+            pl.BlockSpec((None, 1, width), lambda i: (i, 0, 0)),
+            whole((1, width)),
+            whole((1, width)),
+            whole((own_rows, width)),
+            ANY,
+            ANY,
+        ]
+        + [ANY] * len(shards),
+        out_specs=[row_block, row_block, whole((own_rows, width)), whole((own_rows, width)), turned_block, turned_block]
+        + [ANY] * len(shards),
+        out_shape=[full, full, small, small, turned, turned] + full_shapes(shards),
+        scratch_shapes=staging(width) + Gather.semaphores(len(cuts)),
+        compiler_params=pltpu.CompilerParams(
+            collective_id=collective_id, has_side_effects=True, vmem_limit_bytes=60 * 2**20
+        ),
+        name="media_forward",
+    )(feats, embed, gain, bias, own, key_w, value_w, *shards)
+    return outs[:6], [flat_full(o) for o in outs[6:]]
+
+
+def pair_rows(values, first, head):
+    lane = lax.broadcasted_iota(jnp.int32, values.shape, 1)
+    return jnp.concatenate(
+        [
+            jnp.where((lane >= first) & (lane < first + head), values, 0.0),
+            jnp.where((lane >= first + head) & (lane < first + 2 * head), values, 0.0),
+        ],
+        axis=0,
+    )
+
+
+def pair_merge(stacked, first, head):
+    half = stacked.shape[0] // 2
+    lane = lax.broadcasted_iota(jnp.int32, (half, stacked.shape[1]), 1)
+    one = jnp.where((lane >= first) & (lane < first + head), stacked[:half], 0.0)
+    return one + jnp.where((lane >= first + head) & (lane < first + 2 * head), stacked[half:], 0.0)
+
+
+def join(left, right):
+    return jnp.concatenate([left[:, :128], left[:, 128:] + right[:, :128], right[:, 128:]], axis=1)
+
+
+def windows(head):
+    return ((slice(0, 256), 0), (slice(128, 384), 2 * head - 128))
+
+
+def score_block(present, seq, keys, own_keys, q_pair, window, inv_root):
+    at = keys.shape[0]
+    scores = jnp.concatenate([dot(keys[:, window], q_pair, (1, 1)), dot(own_keys[:, window], q_pair, (1, 1))], axis=0)
+    row = lax.broadcasted_iota(jnp.int32, scores.shape, 0)
+    keep = (row >= at) | ((row < at // 2) & (present[seq, 0] > 0)) | ((row >= at // 2) & (present[seq, 1] > 0))
+    return jnp.where(keep, scores * inv_root, MASKED)
+
+
+def attend_kernel(inv_root, head, cuts, steps, *refs):
+    present, queries, keys, values, own_keys, own_values, shard, out, tops, sums, full = refs[:11]
+    seq, group = pl.program_id(0), pl.program_id(1)
+    step = seq * pl.num_programs(1) + group
+    here = Here()
+    moved = Gather(here, [shard], [full], cuts, refs[11:])
+    waves = waves_of(moved)
+    waves[0].insert(0, here.greet)
+    merged = []
+    for p, (window, first) in enumerate(windows(head)):
+        run_tick(step, steps, p, 2, waves)
+        q_pair = pair_rows(queries[:, window], first, head)
+        scores = score_block(present, seq, keys, own_keys, q_pair, window, inv_root)
+        top = jnp.max(scores, axis=0, keepdims=True)
+        expo = jnp.exp(scores - top)
+        tops[pl.ds(group * 2 + p, 1)] = top
+        sums[pl.ds(group * 2 + p, 1)] = jnp.sum(expo, axis=0, keepdims=True)
+        at = keys.shape[0]
+        stacked = dot(expo[:at], values[:, window], (0, 0)) + dot(expo[at:], own_values[:, window], (0, 0))
+        merged.append(pair_merge(stacked, first, head))
+    out[...] = join(*merged)
+    run_last(step, steps, moved)
+
+
+def attend_specs(lat, media, rows):
+    group = 384
+    query = pl.BlockSpec((None, lat, group), lambda b, g: (b, 0, g))
+    key = pl.BlockSpec((media, group), lambda b, g: (b, g))
+    own = pl.BlockSpec((rows, group), lambda b, g: (b, g))
+    stat = pl.BlockSpec((None, 8, 128), lambda b, g: (b, 0, 0))
+    return query, key, own, stat
+
+
+SMEM = pl.BlockSpec(memory_space=pltpu.SMEM)
+
+
+def attend(present, queries, keys, values, own_keys, own_values, shard, pieces, collective_id):
+    seqs, lat, width = queries.shape
+    head = width // HEADS
+    query, key, own, stat = attend_specs(lat, keys.shape[0] // seqs, own_keys.shape[0] // seqs)
+    stat_shape = jax.ShapeDtypeStruct((seqs, 8, 128), F32)
+    cuts = column_cuts([shard.shape[1]], [pieces])
+    grid = (seqs, width // 384)
+    *outs, full = pl.pallas_call(
+        functools.partial(attend_kernel, 1.0 / math.sqrt(head), head, cuts, grid[0] * grid[1]),
+        grid=grid,
+        in_specs=[SMEM, query, key, key, own, own, ANY],
+        out_specs=[query, stat, stat, ANY],
+        out_shape=[jax.ShapeDtypeStruct(queries.shape, F32), stat_shape, stat_shape] + full_shapes([shard]),
+        scratch_shapes=Gather.semaphores(len(cuts)),
+        compiler_params=pltpu.CompilerParams(
+            collective_id=collective_id, has_side_effects=True, vmem_limit_bytes=60 * 2**20
+        ),
+        name="attend",
+    )(present, queries, keys, values, own_keys, own_values, shard)
+    return outs, flat_full(full)
+
+
+def attend_back_kernel(inv_root, head, plan, steps, *refs):
+    present, queries, grads, logs, deltas, keys, values, own_keys, own_values = refs[:9]
+    n = plan.arrays
+    query_out, key_out, value_out, own_key_out, own_value_out = refs[9 + n : 14 + n]
+    seq, group = pl.program_id(0), pl.program_id(1)
+    step = seq * pl.num_programs(1) + group
+    here = Here()
+    moved = plan.bind(here, refs[9 : 9 + n], refs[14 + n : 14 + 2 * n], refs[14 + 2 * n :])
+    waves = waves_of(moved)
+    waves[0].insert(0, here.greet)
+    merged, key_grads, value_grads = [], [], []
+    at = keys.shape[0]
+    for p, (window, first) in enumerate(windows(head)):
+        run_tick(step, steps, p, 2, waves)
+        q_pair = pair_rows(queries[:, window], first, head)
+        g_pair = pair_rows(grads[:, window], first, head)
+        scores = score_block(present, seq, keys, own_keys, q_pair, window, inv_root)
+        probs = jnp.exp(scores - logs[pl.ds(group * 2 + p, 1)])
+        grad_probs = jnp.concatenate(
+            [dot(values[:, window], g_pair, (1, 1)), dot(own_values[:, window], g_pair, (1, 1))], axis=0
+        )
+        grad_scores = probs * (grad_probs - deltas[pl.ds(group * 2 + p, 1)]) * inv_root
+        stacked = dot(grad_scores[:at], keys[:, window], (0, 0)) + dot(grad_scores[at:], own_keys[:, window], (0, 0))
+        merged.append(pair_merge(stacked, first, head))
+        key_grads.append(dot(grad_scores, q_pair))
+        value_grads.append(dot(probs, g_pair))
+    query_out[...] = join(*merged)
+    key_grad, value_grad = join(*key_grads), join(*value_grads)
+    key_out[...], own_key_out[...] = key_grad[:at], key_grad[at:]
+    value_out[...], own_value_out[...] = value_grad[:at], value_grad[at:]
+    run_last(step, steps, moved)
+
+
+def attend_back(present, queries, grads, logs, deltas, keys, values, own_keys, own_values, plan, collective_id):
+    seqs, lat, width = queries.shape
+    head = width // HEADS
+    query, key, own, stat = attend_specs(lat, keys.shape[0] // seqs, own_keys.shape[0] // seqs)
+    shape = lambda v: jax.ShapeDtypeStruct(v.shape, F32)
+    grid = (seqs, width // 384)
+    outs = pl.pallas_call(
+        functools.partial(attend_back_kernel, 1.0 / math.sqrt(head), head, plan, grid[0] * grid[1]),
+        grid=grid,
+        in_specs=[SMEM, query, query, stat, stat, key, key, own, own] + plan.in_specs,
+        out_specs=[query, key, key, own, own] + plan.out_specs,
+        out_shape=[shape(queries), shape(keys), shape(values), shape(own_keys), shape(own_values)] + plan.out_shape,
+        scratch_shapes=plan.scratch,
+        compiler_params=pltpu.CompilerParams(
+            collective_id=collective_id, has_side_effects=True, vmem_limit_bytes=60 * 2**20
+        ),
+        name="attend_back",
+    )(present, queries, grads, logs, deltas, keys, values, own_keys, own_values, *plan.operands)
+    return outs[:5], outs[5:]
+
+
+def weight_kernel(steps, xt_top, xt_low, own, grad_keys, grad_values, own_gk, own_gv, vec, outs, vec_out, mats, *rest):
+    n = pl.program_id(0)
+    here = Here()
+    cut = grad_keys.shape[1]
+    sums = Scatter(
+        here,
+        2 * steps,
+        lambda p: mats.at[p, :, :, :, here.c],
+        lambda p: mats.at[p, :, :, :, here.oc],
+        None,
+        lambda p: outs.at[p % 2, :, pl.ds(pl.multiple_of(p // 2 * cut, cut), cut)],
+        rest[:14],
+    )
+    tot, loc = rest[14:16]
+    small = Scatter(
+        here,
+        1,
+        lambda p: tot,
+        lambda p: vec.at[:, :, :, here.oc],
+        lambda p: pltpu.make_async_copy(vec.at[:, :, :, here.c], tot, loc.at[p]),
+        lambda p: vec_out,
+        rest[16:],
+    )
+    stages = sums.stages()
+
+    @pl.when(n == 0)
+    def _():
+        here.greet()
+
+    own_flat = own[...]
+    for w, (grad, own_grad) in enumerate(((grad_keys, own_gk), (grad_values, own_gv))):
+        pair = halves(grad[...])
+
+        @pl.loop(0, 4)
+        def _(zi):
+            rows = pl.ds(pl.multiple_of(zi * 384, 384), 384)
+            made = dot3((xt_top[rows], xt_low[rows]), pair) + dot(own[:, rows], own_grad[...], (0, 0))
+            mats[2 * n + w, zi] = made.reshape((2, 2, 2, 48, cut))
+
+        sums.start(2 * n + w)
+        for s in (4, 3, 2, 1):
+            p = 2 * n + w - LAG * s
+
+            @pl.when(p >= 0)
+            def _():
+                stages[s](p)
+
+        if w == 1:
+            for s in range(5):
+
+                @pl.when(n == s)
+                def _():
+                    small.stages()[s](0)
+
+    @pl.when(n == steps - 1)
+    def _():
+        for t in range(2 * steps, 2 * steps + 4 * LAG):
+            for s in (4, 3, 2, 1):
+                if 0 <= t - LAG * s < 2 * steps:
+                    stages[s](t - LAG * s)
+
+        @pl.loop(0, 2 * steps)
+        def _(p):
+            sums.done(p)
+
+        small.done(0)
+
+
+def weight_grads(xt_top, xt_low, own, grad_keys, grad_values, own_gk, own_gv, vec, collective_id):
+    width, rows = xt_top.shape
+    own_rows = own.shape[0]
+    steps = width // BLOCK
+    cols = lambda n: pl.BlockSpec((n, BLOCK), lambda i: (0, i))
+    r = width // 32
+    vr, vw = vec.shape[0] // 32, vec.shape[1]
+    outs, vec_sum = pl.pallas_call(
+        functools.partial(weight_kernel, steps),
+        grid=(steps,),
+        in_specs=[
+            whole((width, rows)),
+            whole((width, rows)),
+            whole((own_rows, width)),
+            cols(rows),
+            cols(rows),
+            cols(own_rows),
+            cols(own_rows),
+            ANY,
+        ],
+        out_specs=[whole((2, r, width)), whole((vr, vw))],
+        out_shape=[jax.ShapeDtypeStruct((2, r, width), F32), jax.ShapeDtypeStruct((vr, vw), F32)],
+        scratch_shapes=[pltpu.VMEM((2 * steps,) + GRID + (r, BLOCK), F32)]
+        + Scatter.scratch(2 * steps, r, BLOCK)
+        + [pltpu.VMEM((4, 2, 2, vr, vw), F32), pltpu.SemaphoreType.DMA((1,))]
+        + Scatter.scratch(1, vr, vw),
+        compiler_params=pltpu.CompilerParams(
+            collective_id=collective_id, has_side_effects=True, vmem_limit_bytes=62 * 2**20
+        ),
+        name="weight_grads",
+    )(xt_top, xt_low, own, grad_keys, grad_values, own_gk, own_gv, vec.reshape(GRID + (vr, vw)))
+    return outs[0], outs[1], vec_sum
+
+
+def media_back_kernel(plan, steps, *refs):
+    feats, embed, gain, grad_keys, grad_values, own_gk, own_gv, key_w, value_w = refs[:9]
+    n = plan.arrays
+    out, own_out, sums = refs[9 + n : 12 + n]
+    kt, kl, vt, vl, stage, sems = refs[12 + 2 * n : 18 + 2 * n]
+    step = pl.program_id(0)
+    here = Here()
+    moved = plan.bind(here, refs[9 : 9 + n], refs[12 + n : 12 + 2 * n], refs[18 + 2 * n :])
+    waves = waves_of(moved)
+    waves[0].insert(0, here.greet)
+
+    @pl.when(step == 0)
+    def _():
+        split_weights((key_w, value_w), ((kt, kl), (vt, vl)), stage, sems)
+        own_out[...] = dot3(halves(own_gk[...]), (kt[...], kl[...]), (1, 1)) + dot3(
+            halves(own_gv[...]), (vt[...], vl[...]), (1, 1)
+        )
+        sums[...] = jnp.zeros_like(sums)
+
+    key_pair, value_pair = halves(grad_keys[...]), halves(grad_values[...])
+    for i in range(3):
+        run_tick(step, steps, i, 3, waves)
+        rows = slice(i * 512, i * 512 + 512)
+        out[:, rows] = dot3(key_pair, (kt[rows], kl[rows]), (1, 1)) + dot3(value_pair, (vt[rows], vl[rows]), (1, 1))
+    strip = 64
+
+    @pl.loop(0, out.shape[0] // strip)
+    def _(i):
+        rows = pl.ds(pl.multiple_of(i * strip, strip), strip)
+        incoming = out[rows]
+        unit, inv_std = unit_of(feats[rows] + embed[...])
+        sums[pl.ds(0, 1)] += jnp.sum(incoming * unit, axis=0, keepdims=True)
+        sums[pl.ds(1, 1)] += jnp.sum(incoming, axis=0, keepdims=True)
+        scaled = incoming * gain[...]
+        result = inv_std * (
+            scaled
+            - jnp.mean(scaled, axis=-1, keepdims=True)
+            - unit * jnp.mean(scaled * unit, axis=-1, keepdims=True)
+        )
+        out[rows] = result
+        sums[pl.ds(2 + step, 1)] += jnp.sum(result, axis=0, keepdims=True)
+
+    run_last(step, steps, moved)
+
+
+def media_backward(feats, embed, gain, grad_keys, grad_values, own_gk, own_gv, key_w, value_w, plan, collective_id):
+    rows, width = feats.shape
+    own_rows = own_gk.shape[0]
+    row_block = pl.BlockSpec((BLOCK, width), lambda i: (i, 0))
+    one_block = pl.BlockSpec((BLOCK, width), lambda i: (i, 0), pipeline_mode=pl.Buffered(1))
+    steps = rows // BLOCK
+    outs = pl.pallas_call(
+        functools.partial(media_back_kernel, plan, steps),
+        grid=(steps,),
+        in_specs=[
+            one_block,
+            pl.BlockSpec((None, 1, width), lambda i: (i, 0, 0)),
+            whole((1, width)),
+            row_block,
+            row_block,
+            whole((own_rows, width)),
+            whole((own_rows, width)),
+            ANY,
+            ANY,
+        ]
+        + plan.in_specs,
+        out_specs=[one_block, whole((own_rows, width)), whole((8, width))] + plan.out_specs,
+        out_shape=[
+            jax.ShapeDtypeStruct((rows, width), F32),
+            jax.ShapeDtypeStruct((own_rows, width), F32),
+            jax.ShapeDtypeStruct((8, width), F32),
+        ]
+        + plan.out_shape,
+        scratch_shapes=staging(width) + plan.scratch,
+        compiler_params=pltpu.CompilerParams(
+            collective_id=collective_id, has_side_effects=True, vmem_limit_bytes=64 * 2**20 - 2**16
+        ),
+        name="media_backward",
+    )(feats, embed, gain, grad_keys, grad_values, own_gk, own_gv, key_w, value_w, *plan.operands)
+    return outs[:3], outs[3:]
+
+
+GELU_A = math.sqrt(2.0 / math.pi)
+GELU_B = 0.044715
+
+
+def feed_kernel(feed, cot, up, down, feed_part, new_part, grad_up_t, grad_down):
+    @pl.when(pl.program_id(0) == 0)
+    def _():
+        grad_up_t[...] = jnp.zeros_like(grad_up_t)
+        grad_down[...] = jnp.zeros_like(grad_down)
+
+    hidden = dot(feed[...], up[...])
+    grad_act = dot(cot[...], down[...], (1, 1))
+    square = hidden * hidden
+    bent = jnp.tanh(GELU_A * (hidden + GELU_B * hidden * square))
+    activated = 0.5 * hidden * (1.0 + bent)
+    slope = 0.5 * (1.0 + bent) + 0.5 * hidden * (1.0 - bent * bent) * (GELU_A * (1.0 + 3.0 * GELU_B * square))
+    grad_hidden = grad_act * slope
+    feed_part[...] = dot(grad_hidden, up[...], (1, 1))
+    new_part[...] = dot(activated, down[...])
+    grad_up_t[...] += dot(grad_hidden, feed[...], (0, 0))
+    grad_down[...] += dot(activated, cot[...], (0, 0))
+
+
+def feed_forward(feed, cot, up, down):
+    rows, width = feed.shape
+    units = up.shape[1]
+    row_block = pl.BlockSpec((BLOCK, width), lambda i: (i, 0))
+    one_block = pl.BlockSpec((BLOCK, width), lambda i: (i, 0), pipeline_mode=pl.Buffered(1))
+    big = jax.ShapeDtypeStruct((rows, width), F32)
+    slim = jax.ShapeDtypeStruct((units, width), F32)
+    return pl.pallas_call(
+        feed_kernel,
+        grid=(rows // BLOCK,),
+        in_specs=[row_block, row_block, whole((width, units)), whole((units, width))],
+        out_specs=[row_block, row_block, whole((units, width)), whole((units, width))],
+        out_shape=[big, big, slim, slim],
+        compiler_params=pltpu.CompilerParams(vmem_limit_bytes=60 * 2**20),
+        name="feed_forward",
+    )(feed, cot, up, down)
+
+
+def mm(left, right):
+    return jnp.dot(left, right, precision=HIGH, preferred_element_type=F32)
+
+
+def mm_tn(left, right):
+    return lax.dot_general(left, right, (((0,), (0,)), ((), ())), precision=HIGH, preferred_element_type=F32)
+
+
+def mm_nt(left, right):
+    return lax.dot_general(left, right, (((1,), (1,)), ((), ())), precision=HIGH, preferred_element_type=F32)
+
+
+def body_fast(
+    latents,
+    patch_feats,
+    image_counts,
+    time_index,
+    query_proj,
+    key_proj,
+    value_proj,
+    out_proj,
+    up_proj,
+    down_proj,
+    media_gain,
+    media_bias,
+    latent_gain,
+    latent_bias,
+    feed_gain,
+    feed_bias,
+    time_table,
+    out_cotangent,
+):
+    frame = lax.axis_index("frame")
+    frames = lax.axis_size("frame")
+    seqs, rows, width = latents.shape
+    rounds, patches = patch_feats.shape[1], patch_feats.shape[3]
+    lat = rows * frames
+    head = width // HEADS
+    strip = media_gain.shape[0]
+
+    vectors = jnp.concatenate(
+        [jnp.stack([media_gain, media_bias, latent_gain, latent_bias, feed_gain, feed_bias]), time_table], axis=0
+    )
+    packed = jnp.pad(vectors, ((0, 2), (0, 128 - strip)))
+    (packed_all, key_w, value_w), lat_blocks = gather_first([packed, key_proj, value_proj], [1, 6, 6], latents, 0)
+    vec_all = packed_all.reshape(-1, 16, 128)[:, :14, :strip].transpose(1, 0, 2).reshape(14, width)
+    mgain, mbias, lgain, lbias, fgain, fbias = (vec_all[i] for i in range(6))
+    table = vec_all[6:]
+    up_cols = lax.all_to_all(
+        up_proj.reshape(strip, 32, -1), ("seq", "frame"), split_axis=1, concat_axis=0, tiled=True
+    ).reshape(width, -1)
+
+    latent_all = lat_blocks.reshape(seqs, lat, width)
+    latent_norm, latent_unit, latent_std = norm_forward(latent_all, lgain, lbias)
+    own_rows = lambda v: lax.dynamic_slice_in_dim(v, frame * rows, rows, 1)
+    own_norm, own_unit, own_std = own_rows(latent_norm), own_rows(latent_unit), own_rows(latent_std)
+    slot_ids = jnp.arange(rounds, dtype=jnp.int32) * frames + frame
+    present = slot_ids[None, :] < image_counts[:, None]
+    picks = jnp.arange(time_index.shape[1], dtype=jnp.int32)[None, :] == slot_ids[:, None]
+    slot_times = jnp.sum(jnp.where(picks[None, :, :], time_index[:, None, :], 0), axis=-1)
+    one_hot = slot_times[:, :, None] == jnp.arange(time_table.shape[0], dtype=jnp.int32)
+    slot_embed = jnp.sum(jnp.where(one_hot[..., None], table, 0.0), axis=2)
+    feats = patch_feats.reshape(-1, width)
+    embed = slot_embed.reshape(-1, 1, width)
+    own_flat = flatten(own_norm)
+    (keys, values, own_keys, own_values, xt_top, xt_low), (query_w, cot_all) = media_forward(
+        feats, embed, mgain[None], mbias[None], own_flat, key_w, value_w, [query_proj, flatten(out_cotangent)], [6, 6], 1
+    )
+    queries = mm(flatten(latent_norm), query_w).reshape(seqs, lat, width)
+    present = present.astype(jnp.int32)
+
+    (partial, row_top, row_sum), out_w = attend(
+        present, queries, keys, values, own_keys, own_values, out_proj, 6, 9
+    )
+    stats = jnp.concatenate([row_top.reshape(seqs, HEADS, lat), row_sum.reshape(seqs, HEADS, lat)], axis=1)
+    stats = jnp.pad(stats.transpose(0, 2, 1), ((0, 0), (0, 0), (0, 128 - 2 * HEADS)))
+    part_all, stat_all = group_swap(
+        [partial.reshape(seqs, frames, rows, width), stats.reshape(seqs, frames, rows, 128)], 2
+    )
+    tops, sums = stat_all[..., :HEADS], stat_all[..., HEADS : 2 * HEADS]
+    top = jnp.max(tops, axis=1)
+    ratio = jnp.exp(tops - top[:, None])
+    row_total = jnp.sum(sums * ratio, axis=1)
+    weight = ratio / row_total[:, None]
+    attended = jnp.sum(part_all.reshape(seqs, frames, rows, HEADS, head) * weight[..., None], axis=1)
+    log_total = top + jnp.log(row_total)
+    attended_flat = attended.reshape(seqs, rows, width)
+    middle = latents + mm(flatten(attended_flat), out_w).reshape(seqs, rows, width)
+
+    feed_norm, feed_unit, feed_std = norm_forward(middle, fgain, fbias)
+    (feed_all,) = gather_all([flatten(feed_norm)], [6], 3)
+    feed_part, new_part, grad_up_t, grad_down = feed_forward(feed_all, cot_all, up_cols, down_proj)
+    (grad_feed_norm,) = scatter_all([feed_part], 6, 4)
+    grad_up = lax.all_to_all(
+        grad_up_t.reshape(-1, 32, strip).transpose(1, 2, 0), ("seq", "frame"), split_axis=0, concat_axis=2, tiled=True
+    ).reshape(strip, -1)
+    grad_mid_norm, grad_fgain, grad_fbias = norm_backward(
+        grad_feed_norm.reshape(seqs, rows, width), feed_unit, feed_std, fgain
+    )
+    grad_middle = out_cotangent + grad_mid_norm
+    grad_out_w = mm_tn(flatten(attended_flat), flatten(grad_middle))
+    grad_own = mm_nt(flatten(grad_middle), out_w).reshape(seqs, rows, HEADS, head)
+    delta = jnp.sum(grad_own * attended, axis=-1)
+    back_stats = jnp.pad(jnp.concatenate([log_total, delta], axis=-1), ((0, 0), (0, 0), (0, 128 - 2 * HEADS)))
+    grad_blocks, back_blocks = group_gather([grad_own.reshape(seqs, rows, width), back_stats], 5)
+    back_all = back_blocks.reshape(seqs, lat, 128).transpose(0, 2, 1)
+    logs_all, delta_all = (back_all[:, i * HEADS : (i + 1) * HEADS].reshape(seqs, 8, 128) for i in range(2))
+
+    (query_part, grad_keys, grad_values, own_gk, own_gv), (new_rows,) = attend_back(
+        present,
+        queries,
+        grad_blocks.reshape(seqs, lat, width),
+        logs_all,
+        delta_all,
+        keys,
+        values,
+        own_keys,
+        own_values,
+        Summed([new_part], 6),
+        10,
+    )
+    new_latents = middle + new_rows.reshape(seqs, rows, width)
+    (query_blocks,) = group_swap([query_part.reshape(seqs, frames, rows, width)], 6)
+    grad_queries = flatten(jnp.sum(query_blocks, axis=1))
+
+    grad_query_w = mm_tn(own_flat, grad_queries)
+    (patch_grads, own_back, media_sums), (sum_query, sum_out) = media_backward(
+        feats,
+        embed,
+        mgain[None],
+        grad_keys,
+        grad_values,
+        own_gk,
+        own_gv,
+        key_w,
+        value_w,
+        Summed([grad_query_w, grad_out_w], 6),
+        7,
+    )
+    grad_own_norm = (mm_nt(grad_queries, query_w) + own_back).reshape(seqs, rows, width)
+    grad_lat_in, grad_lgain, grad_lbias = norm_backward(grad_own_norm, own_unit, own_std, lgain)
+    latent_grads = grad_middle + grad_lat_in
+    grad_mgain, grad_mbias = media_sums[0], media_sums[1]
+    slot_sums = media_sums[2:].reshape(seqs, rounds, width)
+    grad_table = jnp.sum(jnp.where(one_hot[..., None], slot_sums[:, :, None, :], 0.0), axis=(0, 1))
+    vec_grads = jnp.concatenate(
+        [jnp.stack([grad_mgain, grad_mbias, grad_lgain, grad_lbias, grad_fgain, grad_fbias]), grad_table], axis=0
+    )
+    vec_blocks = jnp.pad(vec_grads.reshape(14, 32, strip).transpose(1, 0, 2), ((0, 0), (0, 2), (0, 128 - strip)))
+    sum_key, sum_value, sum_vec = weight_grads(
+        xt_top, xt_low, own_flat, grad_keys, grad_values, own_gk, own_gv, vec_blocks.reshape(-1, 128), 8
+    )
+    vec = sum_vec[:14, :strip]
+    return (
+        new_latents,
+        latent_grads,
+        patch_grads.reshape(patch_feats.shape),
+        sum_query,
+        sum_key,
+        sum_value,
+        sum_out,
+        grad_up,
+        grad_down,
+        vec[0],
+        vec[1],
+        vec[2],
+        vec[3],
+        vec[4],
+        vec[5],
+        vec[6:],
+    )
+
+
 def solution(mesh):
+    fast = dict(mesh.shape) == {"seq": 8, "frame": 4}
     return jax.shard_map(
-        body,
+        body_fast if fast else body_general,
         mesh=mesh,
         in_specs=(
             P("seq", "frame", None),

time: 2970 us -> 913 us (0.31)
  waiting for transfers between devices: 1700 us -> 0.01 us
  matrix products: 847 us -> 44.4 us
  Pallas kernels: 0 us -> 784 us
  blocking collectives: 147 us -> 0 us
  local copies, waits for them, and re-layouts: 172 us -> 43.9 us
  other arithmetic: 70.8 us -> 21 us
    reduce_scatter x7 -> x0, waiting for transfers between devices: 1010 us -> none  [the longest x1 356 us: body(): lax.psum_scatter(grad_up, ('seq', 'frame'), scatter_dimension=0, tiled=True)]
    pallas_call x0 -> x12, Pallas kernels: none -> 784 us  [the longest x1 133 us: media_backward(): pl.pallas_call(functools.partial(media_back_kernel, plan, steps), grid=(s...]
    dot_general x49 -> x6, matrix products: 808 us -> 44.4 us  [the longest x2 17.2 us: mm_nt(): lax.dot_general(left, right, (((1,), (1,)), ((), ())), precision=HIGH, pr...]
    all_gather x8 -> x0, waiting for transfers between devices: 664 us -> none  [the longest x1 207 us: body(): lax.all_gather(up_proj, ('seq', 'frame'), axis=0, tiled=True)]
    unnamed x2 -> x0, blocking collectives: 79.4 us -> none
    concatenate x5 -> x8, local copies, waits for them, and re-layouts: 49.3 us -> 0.61 us  [the longest x7 0.5 us: body_fast(): jnp.concatenate([jnp.stack([grad_mgain, grad_mbias, grad_lgain, grad_lbia...]
    all_gather x1 -> x0, blocking collectives: 43.9 us -> none  [body(): lax.all_gather(time_table, ('seq', 'frame'), axis=1, tiled=True)]
    concatenate x2 -> x0, matrix products: 37.2 us -> none  [the longest x1 18.9 us: body(): jnp.concatenate([own_values, media_values.reshape(seq_local, round_count...]
  transfers between devices with their start and end apart: 17 -> 2, of which waited for: 13 -> 0; matrix products, arithmetic and copies ran while one was open for 20% -> 5% of each run, Pallas kernels for 0% -> 53%
where the time goes in v1:
time: 913 us; the launch traced here: 906 us
  Pallas kernels  784 us (86%)
  matrix products  44.4 us (5%)
  local copies, waits for them, and re-layouts  43.9 us (5%)
  other arithmetic  21 us (2%)
  starting transfers between devices  11.4 us (1%)
    pallas_call x1, Pallas kernels, media_backward(): pl.pallas_call(functools.partial(media_back_kernel, plan, steps), grid=(s...  133 us
    pallas_call x1, Pallas kernels, gather_first(): pl.pallas_call(functools.partial(first_kernel, count, cuts), out_shape=fu...  126 us
    pallas_call x1, Pallas kernels, weight_grads(): pl.pallas_call(functools.partial(weight_kernel, steps), grid=(steps,), in...  117 us
    pallas_call x1, Pallas kernels, media_forward(): pl.pallas_call(functools.partial(media_kernel, cuts, rows // BLOCK), grid...  116 us
    pallas_call x1, Pallas kernels, attend_back(): pl.pallas_call(functools.partial(attend_back_kernel, 1.0 / math.sqrt(head...  59.5 us
    pallas_call x1, Pallas kernels, scatter_all(): pl.pallas_call(functools.partial(scatter_kernel, plan), out_shape=plan.ou...  55.4 us
    pallas_call x1, Pallas kernels, attend(): pl.pallas_call(functools.partial(attend_kernel, 1.0 / math.sqrt(head), he...  54.5 us
    pallas_call x1, Pallas kernels, gather_all(): pl.pallas_call(functools.partial(gather_kernel, count, cuts), out_shape=f...  50.7 us
  transfers between devices with their start and end apart: 2, of which 0 were waited for; matrix products, arithmetic and copies ran while one was open for 5% of the time, Pallas kernels for 53%

profile of v1, /device:TPU:0, one launch (start us, length us, event | category | flops | bytes accessed | tf_op | source)
XLA Modules:
  0.0 906.3 jit_solution(2817084887551080449)
XLA Ops:
  2.6 2.1 copy.68
  4.7 7.3 all-to-all-start
  12.8 126.4 %gather_first.1 = (f32[4,2,2,2,16,128]{5,4,3,2,1,0:T(8,128)}, f32[4,2,2,2,48,1536]{5,4,3,2,1,0:T(8,128)}, f32[4,2,2,2,48,1536]{5,4,3,2,1,0:T(8,128)}, f32[3,4,16,1536]{3,2,1,0:T(8,128)}) custom-call(f32[16,128]{1,0:T(8,128)} %pad.16.refs_0_, f32[48,1536]{1,0:T(8,128)} %refs_1_.1, f32[48,1536]{1,0:T(8,128)} %refs_2_.1, f32[3,16,1536]{2,1,0:T(8,128)} %refs_3_.1), custom_call_target="tpu_custom_call" | custom-call | tf_op jit(solution)/shard_map/gather_first/pallas_call | solution.py:695
  150.1 115.6 %media_forward.1 = (f32[1536,1536]{1,0:T(8,128)}, f32[1536,1536]{1,0:T(8,128)}, f32[48,1536]{1,0:T(8,128)}, f32[48,1536]{1,0:T(8,128)}, bf16[1536,1536]{1,0:T(8,...) custom-call(f32[1536,1536]{1,0:T(8,128)} %bitcast.119, ...), custom_call_target="tpu_custom_call" | custom-call | tf_op jit(solution)/shard_map/media_forward/pallas_call | solution.py:987
  265.8 8.2 fusion.9.refs_1_
  274.0 54.5 %attend.1 = (f32[3,64,1536]{2,1,0:T(8,128)}, f32[3,8,128]{2,1,0:T(8,128)}, f32[3,8,128]{2,1,0:T(8,128)}, f32[4,2,2,2,48,1536]{5,4,3,2,1,0:T(8,128)}) custom-call(s32[3,2]{1,0:T(4,128)} %compare_convert_fusion.refs_0_, f32[3,64,1536]{2,1,0:T(8,128)} %fusion.9.refs_1_, f32[1536,1536]{1,0:T(8,128)} %get-tuple-element.58.refs_2_.refs_5_, ...), custom_call_target="tpu_custom_call" | custom-call | tf_op jit(solution)/shard_map/attend/pallas_call | solution.py:1089
  331.0 16.9 %group_swap.2 = (f32[3,4,16,1536]{3,2,1,0:T(8,128)}, f32[3,4,16,128]{3,2,1,0:T(8,128)}) custom-call(f32[3,4,16,1536]{3,2,1,0:T(8,128)} %bitcast.156, f32[3,4,16,128]{3,2,1,0:T(8,128)} %bitcast.161), custom_call_target="tpu_custom_call" | custom-call | tf_op jit(solution)/shard_map/group_swap/pallas_call | solution.py:881
  355.3 6.8 fusion.8
  363.6 50.7 %gather_all.1 = f32[4,2,2,2,48,1536]{5,4,3,2,1,0:T(8,128)} custom-call(f32[48,1536]{1,0:T(8,128)} %bitcast.155), custom_call_target="tpu_custom_call" | custom-call | tf_op jit(solution)/shard_map/gather_all/pallas_call | solution.py:727
  418.4 27.3 %feed_forward.1 = (f32[1536,1536]{1,0:T(8,128)}, f32[1536,1536]{1,0:T(8,128)}, f32[192,1536]{1,0:T(8,128)}, f32[192,1536]{1,0:T(8,128)}) custom-call(f32[1536,1536]{1,0:T(8,128)} %bitcast.129, f32[1536,1536]{1,0:T(8,128)} %bitcast.132, f32[1536,192]{1,0:T(8,128)} %bitcast.136, f32[192,1536]{1,0:T(8,128)} %down.1), custom_call_target="tpu_custom_call" | custom-call | tf_op jit(solution)/shard_map/feed_forward/pallas_call | solution.py:1372
  445.7 55.4 %scatter_all.1 = f32[48,1536]{1,0:T(8,128)} custom-call(f32[4,2,2,2,48,1536]{5,4,3,2,1,0:T(8,128)} %bitcast.131), custom_call_target="tpu_custom_call" | custom-call | tf_op jit(solution)/shard_map/scatter_all/pallas_call | solution.py:789
  504.1 8.1 fusion.10
  513.2 11.6 %group_gather.1 = (f32[3,4,16,1536]{3,2,1,0:T(8,128)}, f32[3,4,16,128]{3,2,1,0:T(8,128)}) custom-call(f32[3,16,1536]{2,1,0:T(8,128)} %bitcast.152, f32[3,16,128]{2,1,0:T(8,128)} %select_maximum_fusion.refs_1_), custom_call_target="tpu_custom_call" | custom-call | tf_op jit(solution)/shard_map/group_gather/pallas_call | solution.py:843
  527.2 59.5 %attend_back.1 = (f32[3,64,1536]{2,1,0:T(8,128)}, f32[1536,1536]{1,0:T(8,128)}, f32[1536,1536]{1,0:T(8,128)}, f32[48,1536]{1,0:T(8,128)}, f32[48,1536]{1,0:T(8,128)}, /*index=5*/f32[48,1536]{1,0:T(8,128)}) custom-call(s32[3,2]{1,0:T(4,128)} %compare_convert_fusion.refs_0_, f32[3,64,1536]{2,1,0:T(8,128)} %fusion.9.refs_1_, f32[3,64,1536]{2,1,0:T(8,128)} %bitcast.154, ...), custom_call_target="tpu_custom_call" | custom-call | tf_op jit(solution)/shard_map/attend_back/pallas_call | solution.py:1143
  586.6 15.6 %group_swap.3 = f32[3,4,16,1536]{3,2,1,0:T(8,128)} custom-call(f32[3,4,16,1536]{3,2,1,0:T(8,128)} %bitcast.157), custom_call_target="tpu_custom_call" | custom-call | tf_op jit(solution)/shard_map/group_swap/pallas_call | solution.py:881
  603.7 6.2 fusion.11.refs_9_
  609.9 6.1 fusion.12.refs_10_
  616.0 133.3 %media_backward.1 = (f32[1536,1536]{1,0:T(8,128)}, f32[48,1536]{1,0:T(8,128)}, f32[8,1536]{1,0:T(8,128)}, f32[48,1536]{1,0:T(8,128)}, f32[48,1536]{1,0:T(8,128)}) custom-call(f32[1536,1536]{1,0:T(8,128)} %bitcast.120, f32[6,1,1536]{2,1,0:T(1,128)} %reshape.346.refs_1_, f32[1,1536]{1,0:T(1,128)} %slice.98.refs_2_, ...), custom_call_target="tpu_custom_call" | custom-call | tf_op jit(solution)/shard_map/media_backward/pallas_call | solution.py:1311
  749.4 9.1 %fusion.5 = (f32[1536]{0:T(1024)S(1)}, f32[1536]{0:T(1024)S(1)}, f32[48]{0:T(128)S(1)}, f32[48,1536]{1,0:T(8,128)}) fusion(f32[3,16,1536]{2,1,0:T(8,128)} %get-tuple-element.163, f32[1536]{0:T(1024)} %copy-done.18, f32[48,1536]{1,0:T(8,128)} %get-tuple-element.79, f32[48,1536]{1,0:T(8,128)} %bitcast.149, f32[1536,1536]{1,0:T(8,128)} %bitcast.126), kind=kOutput, calls=%fused_computation.63 | convolution fusion | flops 679916480 | bytes 10635456 | tf_op jit(solution)/shard_map/dot_general | solution.py:1392
  760.2 4.1 all-to-all-start.1
  766.8 117.2 %weight_grads.1 = (f32[2,48,1536]{2,1,0:T(8,128)}, f32[16,128]{1,0:T(8,128)}) custom-call(bf16[1536,1536]{1,0:T(8,128)(2,1)} %get-tuple-element.82.xt_top, bf16[1536,1536]{1,0:T(8,128)(2,1)} %get-tuple-element.83.xt_low, f32[48,1536]{1,0:T(8,128)} %bitcast.144, f32[1536,1536]{1,0:T(8,128)} %get-tuple-element.75.refs_3_.grad_keys, ...), custom_call_target="tpu_custom_call" | custom-call | tf_op jit(solution)/shard_map/weight_grads/pallas_call | solution.py:1233
  890.6 2.1 copy.74
  892.7 2.8 reshape.380
  895.5 9.1 %copy.91 = f32[3,2,1,256,1536]{4,3,2,1,0:T(8,128)} copy(f32[3,2,1,256,1536]{4,3,2,1,0:T(8,128)} %bitcast.130) | data formatting | bytes 18874368
  (173 shorter events, 48.9 us)
Async XLA Ops:
  4.7 7.4 copy-start.29
  4.7 7.4 copy-start.31
  4.7 7.4 copy-start.32
  4.7 7.4 copy-start.33
  4.7 7.4 copy-start.34
  4.7 7.4 copy-start.35
  4.7 7.4 copy-start.36
  4.7 412.5 %all-to-all-start = ((f32[48,32,192]{2,0,1:T(8,128)}), f32[48,32,192]{2,0,1:T(8,128)S(1)}, u32[]{:S(2)}, u32[]{:S(2)}) async-start(f32[48,32,192]{2,0,1:T(8,128)} %copy.68), calls=%async_computation | async-start | bytes 3145728 | tf_op jit(solution)/shard_map/all_to_all | solution.py:1431
  150.1 115.6 %copy-start.2 = (f32[3,4,16,1536]{3,2,1,0:T(8,128)S(1)}, f32[3,4,16,1536]{3,2,1,0:T(8,128)}, u32[]{:S(2)}) copy-start(f32[3,4,16,1536]{3,2,1,0:T(8,128)} %multiply_add_fusion) | copy-start | bytes 3538948
  363.6 50.7 %copy-start.9 = (f32[3,16,1536]{2,1,0:T(8,128)S(1)}, f32[3,16,1536]{2,1,0:T(8,128)}, u32[]{:S(2)}) copy-start(f32[3,16,1536]{2,1,0:T(8,128)} %get-tuple-element.162) | copy-start | bytes 884740
  504.1 105.8 %copy-start.5 = (f32[3,16,1536]{2,1,0:T(8,128)}, f32[3,16,1536]{2,1,0:T(8,128)S(1)}, u32[]{:S(2)}) copy-start(f32[3,16,1536]{2,1,0:T(8,128)S(1)} %multiply_add_fusion.2) | copy-start | bytes 884740
  603.7 6.2 copy-start.12
  603.7 6.2 copy-start.10
  749.4 9.1 %copy-start.23 = (f32[8,1536]{1,0:T(8,128)S(1)}, f32[8,1536]{1,0:T(8,128)}, u32[]{:S(2)}) copy-start(f32[8,1536]{1,0:T(8,128)} %get-tuple-element.84) | copy-start | bytes 147460
  749.4 9.2 %copy-start.17 = (f32[192,1536]{1,0:T(8,128)S(1)}, f32[192,1536]{1,0:T(8,128)}, u32[]{:S(2)}) copy-start(f32[192,1536]{1,0:T(8,128)} %get-tuple-element.87) | copy-start | bytes 3538948
  760.2 5.4 copy-start.24
  760.2 130.4 %all-to-all-start.1 = ((f32[32,48,192]{2,1,0:T(8,128)}), f32[32,48,192]{2,1,0:T(8,128)S(1)}, u32[]{:S(2)}, u32[]{:S(2)}) async-start(f32[32,48,192]{2,1,0:T(8,128)} %bitcast.135), calls=%async_computation.1 | async-start | bytes 3145728 | tf_op jit(solution)/shard_map/all_to_all | solution.py:1476
  766.8 118.6 %copy-start.7 = (f32[3,16,1536]{2,1,0:T(8,128)S(1)}, f32[3,16,1536]{2,1,0:T(8,128)}, u32[]{:S(2)}) copy-start(f32[3,16,1536]{2,1,0:T(8,128)} %get-tuple-element.163) | copy-start | bytes 884740
  766.8 118.6 %copy-start.19 = (f32[1536]{0:T(1024)S(1)}, f32[1536]{0:T(1024)}, u32[]{:S(2)}) copy-start(f32[1536]{0:T(1024)} %copy-done.18) | copy-start | bytes 18436
  884.0 5.8 copy-start.6
  884.0 5.8 copy-start.13
  884.0 5.8 copy-start.28
  895.5 9.1 %copy-start.22 = (f32[48,1536]{1,0:T(8,128)S(1)}, f32[48,1536]{1,0:T(8,128)}, u32[]{:S(2)}) copy-start(f32[48,1536]{1,0:T(8,128)} %get-tuple-element.202) | copy-start | bytes 884740
  895.5 9.8 %copy-start.21 = (f32[48,1536]{1,0:T(8,128)S(1)}, f32[48,1536]{1,0:T(8,128)}, u32[]{:S(2)}) copy-start(f32[48,1536]{1,0:T(8,128)} %get-tuple-element.205) | copy-start | bytes 884740
  (16 other events, 46.6 us)
